TPU v7x, 256 devices: a whole 4x4x8 slice. The times are simulated.
256 devices in a mesh: island: 8 (over z_hi, core), expert: 32 (over y, z_lo, x).
Axes of the slice: x: 4, y: 4, z: 8 (z_hi: 4, z_lo: 2; z = z_hi * 2 + z_lo), core: 2. Of those that a mesh axis runs over, the one named last changes fastest.
Arguments:
- tokens: bfloat16 [32768, 1792], P(('island', 'expert')), may hold values from -6 to 6
- cotangent: bfloat16 [32768, 1792], P(('island', 'expert')), may hold values from -6 to 6
- route_ids: int32 [32768, 2], P(('island', 'expert')), may hold values from 0 to 15, all different within a row; in each aligned block of 128 rows (0 to 127, 128 to 255, ...) at most 20 rows name the same one
- router_gate_weights: float32 [32768, 2], P(('island', 'expert')), may hold values from 0.1 to 1
- w_gate: bfloat16 [14336, 20480], P('island', 'expert'), may hold values from -0.125 to 0.125
- w_up: bfloat16 [14336, 20480], P('island', 'expert'), may hold values from -0.125 to 0.125
- w_down: bfloat16 [163840, 1792], P(('island', 'expert')), may hold values from -0.15625 to 0.15625
- outer_down: float32 [20480, 1792], P('expert', 'island'), may hold values from -0.15625 to 0.15625
- momentum: float32 [20480, 1792], P('expert', 'island'), may hold values from -0.12 to 0.12
Outputs:
- mixed: bfloat16 [32768, 1792], P(('island', 'expert'))
- input_grad: bfloat16 [32768, 1792], P(('island', 'expert'))
- outer_next: float32 [20480, 1792], P('expert', 'island')
- momentum_next: float32 [20480, 1792], P('expert', 'island')
- fresh_down: bfloat16 [20480, 1792], P('expert')
Inputs may be any that keep to these rules, and one draw needn't show every extreme that they name: `route_ids`: each row names 2 different experts. In each aligned block of 128 rows (the tokens of one device) no expert is named more than 20 times, and in every draw some expert is named exactly 20 times in some block.
All inputs are finite; a program needn't handle non-finite values.
Results may differ from a plain program's by a relative error of at most 0.0064.
Values may be sent and summed in bfloat16 or wider, within the bound.
No kernel may reach another device: no remote copies, remote signals or barrier semaphores. Data moves between devices by JAX's collectives and lax.ppermute only.
A program may use at most 128 MiB of HBM per device.

v0:
```python
import functools

import jax
import jax.numpy as jnp
from jax import lax
from jax.experimental import pallas as pl
from jax.experimental.pallas import tpu as pltpu
from jax.sharding import PartitionSpec as P

NX = 4
N_YZ = 8
CORES = 2
NZ = 4

inner_rate = 0.001
outer_rate = 0.7
outer_beta = 0.9

F32 = jnp.float32
BF16 = jnp.bfloat16
FIRST = (((0,), (0,)), ((), ()))
LAST = (((1,), (1,)), ((), ()))

VMEM = pl.BlockSpec(memory_space=pltpu.VMEM)
SMEM = pl.BlockSpec(memory_space=pltpu.SMEM)


def call(kernel, out_shape, args, smem=0, after=(), scratch=(), name=None):
    args, after = list(args), list(after)
    count, skipped = len(args), len(after)

    def body(*refs):
        kernel(*refs[:count], *refs[count + skipped :])

    return pl.pallas_call(
        body,
        out_shape=out_shape,
        in_specs=[SMEM] * smem + [VMEM] * (count - smem) + [pl.BlockSpec(memory_space=pl.ANY)] * skipped,
        out_specs=jax.tree.map(lambda _: VMEM, out_shape),
        scratch_shapes=scratch,
        compiler_params=pltpu.CompilerParams(vmem_limit_bytes=60 * 1024 * 1024),
        name=name,
    )(*args, *after)


def shape(rows, columns, dtype):
    return jax.ShapeDtypeStruct((rows, columns), dtype)


def pick_masks(routes, xp, capacity):
    tokens = routes.shape[1]
    slots = 2 * N_YZ * capacity
    first, second = routes[0:1, :], routes[1:2, :]
    expert = lax.broadcasted_iota(jnp.int32, (2 * N_YZ, tokens), 0)
    named = ((expert == first) | (expert == second)).astype(BF16)
    earlier = (
        lax.broadcasted_iota(jnp.int32, (tokens, tokens), 0)
        < lax.broadcasted_iota(jnp.int32, (tokens, tokens), 1)
    ).astype(BF16)
    before = jnp.dot(named, earlier, preferred_element_type=F32)
    where = lax.broadcasted_iota(jnp.int32, (slots, tokens), 0)

    def mask(ids):
        slot = jnp.sum(jnp.where(expert == ids, before, 0.0), axis=0, keepdims=True).astype(jnp.int32)
        place = (ids >> 1) * (2 * capacity) + jnp.where((ids & 1) == xp, 0, capacity) + slot
        return where == place

    return mask(first), mask(second)


def as_bf16(mask):
    return jnp.where(mask, 1.0, 0.0).astype(BF16)


def pack_tokens(capacity, half_ref, route_ref, tokens_ref, out_ref):
    one, two = pick_masks(route_ref[...], half_ref[0], capacity)
    chosen = jnp.dot(as_bf16(one | two), tokens_ref[...], preferred_element_type=F32)
    out_ref[...] = chosen.astype(BF16)


def pack_scores(capacity, half_ref, route_ref, gate_ref, cotangent_ref, out_ref):
    one, two = pick_masks(route_ref[...], half_ref[0], capacity)
    gates = gate_ref[...]
    weights = jnp.where(one, gates[0:1, :], 0.0) + jnp.where(two, gates[1:2, :], 0.0)
    weight = jnp.sum(weights, axis=1, keepdims=True)
    chosen = jnp.dot(as_bf16(one | two), cotangent_ref[...], preferred_element_type=F32)
    out_ref[...] = (weight * chosen).astype(BF16)


def split_rows(capacity, got_ref, own_ref, other_ref):
    for b in range(N_YZ):
        rows = pl.ds(b * capacity, capacity)
        own_ref[rows, :] = got_ref[pl.ds(2 * b * capacity, capacity), :]
        other_ref[rows, :] = got_ref[pl.ds((2 * b + 1) * capacity, capacity), :]


def merge_rows(capacity, mine_ref, theirs_ref, other_ref, out_ref):
    for b in range(N_YZ):
        rows = pl.ds(b * capacity, capacity)
        whole = mine_ref[rows, :].astype(F32) + theirs_ref[rows, :].astype(F32)
        out_ref[pl.ds(2 * b * capacity, capacity), :] = whole.astype(BF16)
        out_ref[pl.ds((2 * b + 1) * capacity, capacity), :] = other_ref[rows, :]


def add_rows(mine_ref, theirs_ref, out_ref):
    out_ref[...] = (mine_ref[...].astype(F32) + theirs_ref[...].astype(F32)).astype(BF16)


def forward(x0, x1, x2, x3, gate_ref, up_ref, hidden_ref, slope_ref, act_ref):
    rows = x0.shape[0]
    for c, x in enumerate((x0, x1, x2, x3)):
        chunk = pl.ds(c * rows, rows)
        block = x[...]
        gate_pre = jnp.dot(block, gate_ref[...], preferred_element_type=F32)
        up_pre = jnp.dot(block, up_ref[...], preferred_element_type=F32)
        sigmoid_a = jax.nn.sigmoid(gate_pre)
        activated = gate_pre * sigmoid_a
        hidden_ref[chunk, :] = (activated * up_pre).astype(BF16)
        slope_ref[chunk, :] = up_pre * sigmoid_a * (1.0 + gate_pre * (1.0 - sigmoid_a))
        act_ref[chunk, :] = activated


def down(hidden_ref, down_ref, o0, o1, o2, o3):
    rows = o0.shape[0]
    for c, out in enumerate((o0, o1, o2, o3)):
        block = hidden_ref[pl.ds(c * rows, rows), :]
        out[...] = jnp.dot(block, down_ref[...], preferred_element_type=F32).astype(BF16)


def backward(first, s0, s1, gate_ref, up_ref, down_ref, slope_ref, act_ref, o0, o1):
    rows = s0.shape[0]
    for c, (s, out) in enumerate(((s0, o0), (s1, o1))):
        chunk = pl.ds((first + c) * rows, rows)
        grad_hidden = lax.dot_general(s[...], down_ref[...], LAST, preferred_element_type=F32)
        grad_gate = (grad_hidden * slope_ref[chunk, :]).astype(BF16)
        grad_up = (grad_hidden * act_ref[chunk, :]).astype(BF16)
        out[...] = (
            lax.dot_general(grad_gate, gate_ref[...], LAST, preferred_element_type=F32)
            + lax.dot_general(grad_up, up_ref[...], LAST, preferred_element_type=F32)
        ).astype(BF16)


def inner_step(place_ref, s0, s1, s2, s3, hidden_ref, down_ref, mine_ref, theirs_ref, whole_ref):
    rows = s0.shape[0]
    total = None
    for c, s in enumerate((s0, s1, s2, s3)):
        part = lax.dot_general(s[...], hidden_ref[pl.ds(c * rows, rows), :], FIRST, preferred_element_type=F32)
        total = part if total is None else total + part
    whole_ref[...] = down_ref[...].astype(F32).T - inner_rate * total
    block = mine_ref.shape[0] // NZ
    z, core = place_ref[0], place_ref[1]
    for d in range(NZ):
        at = lax.rem(z + d, NZ) * CORES
        mine_ref[pl.ds(d * block, block), :] = whole_ref[pl.ds(pl.multiple_of((at + core) * block, 8), block), :]
        theirs_ref[pl.ds(d * block, block), :] = whole_ref[
            pl.ds(pl.multiple_of((at + 1 - core) * block, 8), block), :
        ].astype(BF16)


def core_sum(mine_ref, theirs_ref, own_ref, before_ref, after_ref, far_low_ref, far_high_ref):
    block = own_ref.shape[0]
    half = block // 2

    def total(start, count):
        rows = pl.ds(start, count)
        return mine_ref[rows, :] + theirs_ref[rows, :].astype(F32)

    own_ref[...] = total(0, block)
    after_ref[...] = total(block, block)
    far_low_ref[...] = total(2 * block, half).astype(BF16)
    far_high_ref[...] = total(2 * block + half, half).astype(BF16)
    before_ref[...] = total(3 * block, block)


def ring_sum(before_ref, after_ref, low_ref, high_ref, to_next_ref, to_last_ref):
    half = low_ref.shape[0]
    low, high = pl.ds(0, half), pl.ds(half, half)
    to_next_ref[low, :] = (after_ref[low, :] + low_ref[...].astype(F32)).astype(BF16)
    to_next_ref[high, :] = after_ref[high, :].astype(BF16)
    to_last_ref[low, :] = before_ref[low, :].astype(BF16)
    to_last_ref[high, :] = (before_ref[high, :] + high_ref[...].astype(F32)).astype(BF16)


def outer_step(islands, own_ref, left_ref, right_ref, outer_ref, momentum_ref, next_ref, moved_ref, fresh_ref):
    total = own_ref[...] + left_ref[...].astype(F32) + right_ref[...].astype(F32)
    outer_down = outer_ref[...]
    mean_delta = outer_down - total.T / islands
    momentum_next = outer_beta * momentum_ref[...] + mean_delta
    outer_next = outer_down - outer_rate * (mean_delta + outer_beta * momentum_next)
    next_ref[...] = outer_next
    moved_ref[...] = momentum_next
    fresh_ref[...] = outer_next.T.astype(BF16)


def assemble(place_ref, *refs):
    *parts, out_ref, whole_ref = refs
    z, core = place_ref[0], place_ref[1]
    block = parts[0].shape[0]
    for side in range(CORES):
        own, after, low, high, before = parts[5 * side : 5 * side + 5]
        column = core if side == 0 else 1 - core

        def start(d):
            return pl.multiple_of((lax.rem(z + d, NZ) * CORES + column) * block, 16)

        whole_ref[pl.ds(start(0), block), :] = own[...].astype(F32)
        whole_ref[pl.ds(start(1), block), :] = after[...].astype(F32)
        whole_ref[pl.ds(start(2), block // 2), :] = low[...].astype(F32)
        whole_ref[pl.ds(start(2) + block // 2, block // 2), :] = high[...].astype(F32)
        whole_ref[pl.ds(start(3), block), :] = before[...].astype(F32)
    out_ref[...] = whole_ref[...].T.astype(BF16)


def mix(capacity, half_ref, route_ref, gate_ref, rows_ref, out_ref):
    one, two = pick_masks(route_ref[...], half_ref[0], capacity)
    rows = rows_ref[...]
    gates = gate_ref[...].T
    out_ref[...] = (
        gates[:, 0:1] * lax.dot_general(as_bf16(one), rows, FIRST, preferred_element_type=F32)
        + gates[:, 1:2] * lax.dot_general(as_bf16(two), rows, FIRST, preferred_element_type=F32)
    ).astype(BF16)


def gather_grad(capacity, half_ref, route_ref, rows_ref, out_ref):
    one, two = pick_masks(route_ref[...], half_ref[0], capacity)
    out_ref[...] = lax.dot_general(as_bf16(one | two), rows_ref[...], FIRST, preferred_element_type=F32).astype(BF16)


def per_device(tokens, cotangent, route_ids, gates, w_gate, w_up, w_down, outer_down, momentum):
    groups = lax.axis_size("expert")
    islands = lax.axis_size("island")
    token_count, top_count = route_ids.shape
    features = tokens.shape[1]
    hidden_count = w_gate.shape[1]
    experts = groups // 2
    capacity = 5 * token_count * top_count // (4 * experts)
    slots = experts * capacity
    half_rows = slots // 2
    n = outer_down.shape[1]
    h = n // 2

    place = lax.axis_index("expert")
    island = lax.axis_index("island")
    xp = ((place % NX) // 2).astype(jnp.int32).reshape(1)
    at = jnp.stack([island // CORES, island % CORES]).astype(jnp.int32)

    pair = [(i, i ^ 1) for i in range(groups)]
    across = [(i, i ^ 3) for i in range(groups)]
    same_x = [[b * NX + x for b in range(N_YZ)] for x in range(NX)]
    other_core = [(i, i ^ 1) for i in range(islands)]
    ahead = [(i, (i + CORES) % islands) for i in range(islands)]
    behind = [(i, (i - CORES) % islands) for i in range(islands)]

    def to_pair(v):
        return lax.ppermute(v, "expert", pair)

    def to_across(v):
        return lax.ppermute(v, "expert", across)

    def by_z(v, perm):
        return lax.ppermute(v, "island", perm)

    def exchange(v):
        v = v.reshape(N_YZ, 2 * capacity, features)
        v = lax.all_to_all(v, "expert", split_axis=0, concat_axis=0, tiled=True, axis_index_groups=same_x)
        return v.reshape(slots, features)

    part = functools.partial
    half_shape = shape(half_rows, features, BF16)
    whole_shape = shape(slots, features, BF16)
    routes, weights = route_ids.T, gates.T

    packed_x = call(part(pack_tokens, capacity), whole_shape, [xp, routes, tokens], smem=1, name="pack_tokens")
    packed_s = call(
        part(pack_scores, capacity),
        whole_shape,
        [xp, routes, weights, cotangent],
        smem=1,
        after=[packed_x],
        name="pack_scores",
    )
    own_x, other_x = call(part(split_rows, capacity), (half_shape,) * 2, [exchange(packed_x)], name="split_x")
    crossed_x = to_across(other_x)
    xs = (own_x, crossed_x, to_pair(own_x), to_pair(crossed_x))
    own_s, other_s = call(
        part(split_rows, capacity), (half_shape,) * 2, [exchange(packed_s)], after=[own_x], name="split_s"
    )
    crossed_s = to_across(other_s)
    ss = (own_s, crossed_s, to_pair(own_s), to_pair(crossed_s))

    total_rows = 2 * slots
    hidden, slope, activated = call(
        forward,
        (
            shape(total_rows, hidden_count, BF16),
            shape(total_rows, hidden_count, F32),
            shape(total_rows, hidden_count, F32),
        ),
        [*xs, w_gate, w_up],
        after=[own_s],
        name="forward",
    )
    outs = call(down, (half_shape,) * 4, [hidden, w_down], after=[ss[2]], name="down")

    half_features = NZ * n
    mine, theirs = call(
        inner_step,
        (shape(half_features, hidden_count, F32), shape(half_features, hidden_count, BF16)),
        [at, *ss, hidden, w_down],
        smem=1,
        after=[outs[0]],
        scratch=[pltpu.VMEM((features, hidden_count), F32)],
        name="inner_step",
    )
    from_core = by_z(theirs, other_core)

    far_ins = call(
        part(backward, 2),
        (half_shape,) * 2,
        [ss[2], ss[3], w_gate, w_up, w_down, slope, activated],
        after=[theirs],
        name="backward_far",
    )
    block32, blockb, halfb = shape(n, hidden_count, F32), shape(n, hidden_count, BF16), shape(h, hidden_count, BF16)
    own_sum, before, after, far_low, far_high = call(
        core_sum, (block32,) * 3 + (halfb,) * 2, [mine, from_core], after=[far_ins[0]], name="core_sum"
    )
    near_ins = call(
        part(backward, 0),
        (half_shape,) * 2,
        [ss[0], ss[1], w_gate, w_up, w_down, slope, activated],
        after=[far_low],
        name="backward_near",
    )

    sum_out = call(add_rows, half_shape, [outs[1], to_pair(outs[3])], after=[near_ins[0]], name="sum_out")
    to_next, to_last = call(
        ring_sum,
        (blockb,) * 2,
        [before, after, by_z(far_low, ahead), by_z(far_high, behind)],
        after=[sum_out],
        name="ring_sum",
    )
    merged_out = call(
        part(merge_rows, capacity),
        whole_shape,
        [outs[0], to_pair(outs[2]), to_across(sum_out)],
        after=[to_next],
        name="merge_out",
    )
    sum_in = call(add_rows, half_shape, [near_ins[1], to_pair(far_ins[1])], after=[merged_out], name="sum_in")
    outer_next, momentum_next, fresh = call(
        part(outer_step, islands),
        (shape(hidden_count, n, F32), shape(hidden_count, n, F32), blockb),
        [own_sum, by_z(to_next, ahead), by_z(to_last, behind), outer_down, momentum],
        after=[sum_in],
        name="outer_step",
    )
    mixed = call(
        part(mix, capacity),
        shape(token_count, features, BF16),
        [xp, routes, weights, exchange(merged_out)],
        smem=1,
        after=[fresh],
        name="mix",
    )
    merged_in = call(
        part(merge_rows, capacity),
        whole_shape,
        [near_ins[0], to_pair(far_ins[0]), to_across(sum_in)],
        after=[mixed],
        name="merge_in",
    )
    left = by_z(fresh, ahead)
    right = by_z(fresh, behind)
    low = by_z(left[:h], ahead)
    high = by_z(right[h:], behind)
    blocks = [fresh, right, low, high, left]
    blocks += [by_z(b, other_core) for b in blocks]
    fresh_down = call(
        assemble,
        shape(hidden_count, features, BF16),
        [at, *blocks],
        smem=1,
        after=[merged_in],
        scratch=[pltpu.VMEM((features, hidden_count), F32)],
        name="assemble",
    )
    input_grad = call(
        part(gather_grad, capacity),
        shape(token_count, features, BF16),
        [xp, routes, exchange(merged_in)],
        smem=1,
        after=[fresh_down],
        name="gather_grad",
    )
    return mixed, input_grad, outer_next, momentum_next, fresh_down


def solution(mesh):
    rows = P(("island", "expert"), None)
    columns = P("expert", "island")
    return jax.shard_map(
        per_device,
        mesh=mesh,
        in_specs=(rows, rows, rows, rows, P("island", "expert"), P("island", "expert"), rows, columns, columns),
        out_specs=(rows, rows, columns, columns, P("expert", None)),
        check_vma=False,
    )
```

profile of v0, /device:TPU:1, one launch (start us, length us, event | category | flops | bytes accessed | tf_op | source)
XLA Modules:
  0.0 264.9 jit_solution(16536023428967441657)
XLA Ops:
  0.7 2.6 pack_tokens.1.refs_4_
  3.3 6.4 %all-to-all-start = ((bf16[8,40,1792]{2,1,0:T(8,128)(2,1)}), bf16[8,40,1792]{2,1,0:T(8,128)(2,1)S(1)}, u32[]{:S(2)}, u32[]{:S(2)}) async-start(bf16[8,40,1792]{2,1,0:T(8,128)(2,1)} %bitcast.15), calls=%async_computation | async-start | bytes 2293760 | tf_op jit(solution)/shard_map/all_to_all | solution.py:265
  9.7 2.7 %pack_scores.1 = bf16[320,1792]{1,0:T(8,128)(2,1)} custom-call(s32[1]{0:T(128)} %bitcast.refs_0_, s32[2,128]{1,0:T(2,128)} %bitcast.22, f32[2,128]{1,0:T(2,128)} %bitcast.25, bf16[128,1792]{1,0:T(8,128)(2,1)} %refs_3_.4, bf16[320,1792]{1,0:T(8,128)(2,1)} %pack_tokens.1.refs_4_), custom_call_target="tpu_custom_call" | custom-call | tf_op jit(solution)/shard_map/pack_scores/pallas_call | solution.py:35
  12.4 13.2 %all-to-all-done = bf16[8,40,1792]{2,1,0:T(8,128)(2,1)S(1)} async-done(((bf16[8,40,1792]{2,1,0:T(8,128)(2,1)}), bf16[8,40,1792]{2,1,0:T(8,128)(2,1)S(1)}, u32[]{:S(2)}, u32[]{:S(2)}) %all-to-all-start) | async-done | bytes 1146912 | tf_op jit(solution)/shard_map/all_to_all | solution.py:265
  26.6 3.8 %all-to-all-start.1 = ((bf16[8,40,1792]{2,1,0:T(8,128)(2,1)}), bf16[8,40,1792]{2,1,0:T(8,128)(2,1)S(1)}, u32[]{:S(2)}, u32[]{:S(2)}) async-start(bf16[8,40,1792]{2,1,0:T(8,128)(2,1)} %bitcast.20), calls=%async_computation.1 | async-start | bytes 2293760 | tf_op jit(solution)/shard_map/all_to_all | solution.py:265
  30.3 2.4 split_x.1
  32.7 2.5 collective-permute-start
  35.2 10.1 %all-to-all-done.1 = bf16[8,40,1792]{2,1,0:T(8,128)(2,1)S(1)} async-done(((bf16[8,40,1792]{2,1,0:T(8,128)(2,1)}), bf16[8,40,1792]{2,1,0:T(8,128)(2,1)S(1)}, u32[]{:S(2)}, u32[]{:S(2)}) %all-to-all-start.1) | async-done | bytes 1146912 | tf_op jit(solution)/shard_map/all_to_all | solution.py:265
  46.2 2.4 split_s.1
  48.6 2.5 collective-permute-start.6
  52.7 9.0 %collective-permute-done.6.refs_2_.refs_1_ = bf16[160,1792]{1,0:T(8,128)(2,1)S(1)} collective-permute-done((bf16[160,1792]{1,0:T(8,128)(2,1)}, bf16[160,1792]{1,0:T(8,128)(2,1)S(1)}, u32[]{:S(2)}, u32[]{:S(2)}) %collective-permute-start.6) | collective-permute-done | bytes 573472 | tf_op jit(solution)/shard_map/ppermute | solution.py:258
  62.6 12.3 %collective-permute-done.2.refs_3_ = bf16[160,1792]{1,0:T(8,128)(2,1)} collective-permute-done((bf16[160,1792]{1,0:T(8,128)(2,1)S(1)}, bf16[160,1792]{1,0:T(8,128)(2,1)}, u32[]{:S(2)}, u32[]{:S(2)}) %collective-permute-start.2) | collective-permute-done | bytes 573472 | tf_op jit(solution)/shard_map/ppermute | solution.py:255
  74.9 8.8 %forward.1 = (bf16[640,640]{1,0:T(8,128)(2,1)}, f32[640,640]{1,0:T(8,128)}, f32[640,640]{1,0:T(8,128)}) custom-call(bf16[160,1792]{1,0:T(8,128)(2,1)} %get-tuple-element.32.refs_1_.refs_0_, bf16[160,1792]{1,0:T(8,128)(2,1)} %copy-done.14, bf16[160,1792]{1,0:T(8,128)(2,1)} %copy-done.15, bf16[160,1792]{1,0:T(8,128)(2,1)} %collective-permute-done.2.refs_3_, ...), custom_call_target="tpu_custom_call" | custom-call | tf_op jit(solution)/shard_map/forward/pallas_call | solution.py:35
  83.7 3.3 %collective-permute-done.3.refs_2_.refs_3_.refs_0_ = bf16[160,1792]{1,0:T(8,128)(2,1)S(1)} collective-permute-done((bf16[160,1792]{1,0:T(8,128)(2,1)}, bf16[160,1792]{1,0:T(8,128)(2,1)S(1)}, u32[]{:S(2)}, u32[]{:S(2)}) %collective-permute-start.3) | collective-permute-done | bytes 573472 | tf_op jit(solution)/shard_map/ppermute | solution.py:255
  87.9 4.7 %down.1 = (bf16[160,1792]{1,0:T(8,128)(2,1)}, bf16[160,1792]{1,0:T(8,128)(2,1)}, bf16[160,1792]{1,0:T(8,128)(2,1)}, bf16[160,1792]{1,0:T(8,128)(2,1)}) custom-call(bf16[640,640]{1,0:T(8,128)(2,1)} %get-tuple-element.35.refs_0_.refs_5_, bf16[640,1792]{1,0:T(8,128)(2,1)} %refs_4_.6, bf16[160,1792]{1,0:T(8,128)(2,1)} %copy-done), custom_call_target="tpu_custom_call" | custom-call | tf_op jit(solution)/shard_map/down/pallas_call | solution.py:35
  92.6 6.8 %collective-permute-done.7.refs_4_.refs_1_ = bf16[160,1792]{1,0:T(8,128)(2,1)S(1)} collective-permute-done((bf16[160,1792]{1,0:T(8,128)(2,1)S(1)}, bf16[160,1792]{1,0:T(8,128)(2,1)S(1)}, u32[]{:S(2)}, u32[]{:S(2)}) %collective-permute-start.7) | collective-permute-done | bytes 573472 | tf_op jit(solution)/shard_map/ppermute | solution.py:255
  100.2 7.8 %inner_step.1 = (f32[896,640]{1,0:T(8,128)}, bf16[896,640]{1,0:T(8,128)(2,1)}) custom-call(s32[2]{0:T(128)} %pad_add_fusion.refs_0_, bf16[160,1792]{1,0:T(8,128)(2,1)} %get-tuple-element.34.refs_6_.refs_1_.refs_0_, bf16[160,1792]{1,0:T(8,128)(2,1)} %copy-done.5, bf16[160,1792]{1,0:T(8,128)(2,1)} %copy-done, bf16[160,1792]{1,0:T(8,128)(2,1)} %copy-done.6, ...), custom_call_target="tpu_custom_call" | custom-call | tf_op jit(solution)/shard_map/inner_step/pallas_call | solution.py:35
  108.0 4.0 %collective-permute-start.8 = (bf16[896,640]{1,0:T(8,128)(2,1)}, bf16[896,640]{1,0:T(8,128)(2,1)S(1)}, u32[]{:S(2)}, u32[]{:S(2)}) collective-permute-start(bf16[896,640]{1,0:T(8,128)(2,1)} %get-tuple-element.44.refs_7_), channel_id=1, source_target_pairs={{0,32},{32,0},{64,96},{96,64},{128,160},{160,128},{192,224},{224,1... | collective-permute-start | bytes 3440648 | tf_op jit(solution)/shard_map/ppermute | solution.py:261
  112.0 1.7 collective-permute-start.4
  113.7 9.9 %backward_far.1 = (bf16[160,1792]{1,0:T(8,128)(2,1)}, bf16[160,1792]{1,0:T(8,128)(2,1)}) custom-call(bf16[160,1792]{1,0:T(8,128)(2,1)} %copy-done, bf16[160,1792]{1,0:T(8,128)(2,1)} %copy-done.6, bf16[1792,640]{1,0:T(8,128)(2,1)} %refs_2_.5, bf16[1792,640]{1,0:T(8,128)(2,1)} %refs_3_.6, bf16[640,1792]{1,0:T(8,128)(2,1)} %refs_4_.6, ...), custom_call_target="tpu_custom_call" | custom-call | tf_op jit(solution)/shard_map/backward_far/pallas_call | solution.py:35
  124.6 3.2 %core_sum.1 = (f32[224,640]{1,0:T(8,128)}, f32[224,640]{1,0:T(8,128)}, f32[224,640]{1,0:T(8,128)}, bf16[112,640]{1,0:T(8,128)(2,1)}, bf16[112,640]{1,0:T(8,128)(2,1)}) custom-call(f32[896,640]{1,0:T(8,128)} %get-tuple-element.43.refs_0_, bf16[896,640]{1,0:T(8,128)(2,1)} %copy-done.9, bf16[160,1792]{1,0:T(8,128)(2,1)} %get-tuple-element.45.refs_2_), custom_call_target="tpu_custom_call" | custom-call | tf_op jit(solution)/shard_map/core_sum/pallas_call | solution.py:35
  127.9 9.9 %backward_near.1 = (bf16[160,1792]{1,0:T(8,128)(2,1)}, bf16[160,1792]{1,0:T(8,128)(2,1)}) custom-call(bf16[160,1792]{1,0:T(8,128)(2,1)} %get-tuple-element.34.refs_6_.refs_1_.refs_0_, bf16[160,1792]{1,0:T(8,128)(2,1)} %copy-done.5, bf16[1792,640]{1,0:T(8,128)(2,1)} %refs_2_.5, bf16[1792,640]{1,0:T(8,128)(2,1)} %refs_3_.6, bf16[640,1792]{1,0:T(8,128)(2,1)} %refs_4_.6, ...), custom_call_target="tpu_custom_call" | custom-call | tf_op jit(solution)/shard_map/backward_near/pallas_call | solution.py:35
  138.6 2.2 sum_out.1.refs_4_
  141.0 3.0 %collective-permute-start.10 = (bf16[112,640]{1,0:T(8,128)(2,1)S(1)}, bf16[112,640]{1,0:T(8,128)(2,1)S(1)}, u32[]{:S(2)}, u32[]{:S(2)}) collective-permute-start(bf16[112,640]{1,0:T(8,128)(2,1)S(1)} %copy-done.24), channel_id=1, source_target_pairs={{0,64},{32,96},{64,128},{96,160},{128,192},{160,224},{192,0},{224,... | collective-permute-start | bytes 430088 | tf_op jit(solution)/shard_map/ppermute | solution.py:261
  144.0 2.2 collective-permute-start.11
  146.2 3.9 %collective-permute-done.10.refs_2_ = bf16[112,640]{1,0:T(8,128)(2,1)S(1)} collective-permute-done((bf16[112,640]{1,0:T(8,128)(2,1)S(1)}, bf16[112,640]{1,0:T(8,128)(2,1)S(1)}, u32[]{:S(2)}, u32[]{:S(2)}) %collective-permute-start.10) | collective-permute-done | bytes 143392 | tf_op jit(solution)/shard_map/ppermute | solution.py:261
  150.2 4.1 %collective-permute-done.11.refs_3_ = bf16[112,640]{1,0:T(8,128)(2,1)S(1)} collective-permute-done((bf16[112,640]{1,0:T(8,128)(2,1)S(1)}, bf16[112,640]{1,0:T(8,128)(2,1)S(1)}, u32[]{:S(2)}, u32[]{:S(2)}) %collective-permute-start.11) | collective-permute-done | bytes 143392 | tf_op jit(solution)/shard_map/ppermute | solution.py:261
  154.9 2.1 ring_sum.1
  158.1 2.6 merge_out.1.refs_2_
  160.7 3.7 %all-to-all-start.2 = ((bf16[8,40,1792]{2,1,0:T(8,128)(2,1)}), bf16[8,40,1792]{2,1,0:T(8,128)(2,1)S(1)}, u32[]{:S(2)}, u32[]{:S(2)}) async-start(bf16[8,40,1792]{2,1,0:T(8,128)(2,1)} %bitcast.13), calls=%async_computation.2 | async-start | bytes 2293760 | tf_op jit(solution)/shard_map/all_to_all | solution.py:265
  166.0 11.3 %collective-permute-done.14.refs_1_ = bf16[160,1792]{1,0:T(8,128)(2,1)S(1)} collective-permute-done((bf16[160,1792]{1,0:T(8,128)(2,1)S(1)}, bf16[160,1792]{1,0:T(8,128)(2,1)S(1)}, u32[]{:S(2)}, u32[]{:S(2)}) %collective-permute-start.14) | collective-permute-done | bytes 573472 | tf_op jit(solution)/shard_map/ppermute | solution.py:255
  178.1 2.2 sum_in.1.refs_5_
  180.3 2.5 collective-permute-start.16
  182.8 4.0 %collective-permute-start.12 = (bf16[224,640]{1,0:T(8,128)(2,1)}, bf16[224,640]{1,0:T(8,128)(2,1)}, u32[]{:S(2)}, u32[]{:S(2)}) collective-permute-start(bf16[224,640]{1,0:T(8,128)(2,1)} %get-tuple-element.51.refs_3_), channel_id=1, source_target_pairs={{0,64},{32,96},{64,128},{96,160},{128,192},{160,224},{192,0},{224,... | collective-permute-start | bytes 860168 | tf_op jit(solution)/shard_map/ppermute | solution.py:261
  189.2 7.6 %collective-permute-done.12.refs_1_ = bf16[224,640]{1,0:T(8,128)(2,1)} collective-permute-done((bf16[224,640]{1,0:T(8,128)(2,1)}, bf16[224,640]{1,0:T(8,128)(2,1)}, u32[]{:S(2)}, u32[]{:S(2)}) %collective-permute-start.12) | collective-permute-done | bytes 286752 | tf_op jit(solution)/shard_map/ppermute | solution.py:261
  197.4 3.1 %outer_step.1 = (f32[640,224]{1,0:T(8,128)}, f32[640,224]{1,0:T(8,128)}, bf16[224,640]{1,0:T(8,128)(2,1)}) custom-call(f32[224,640]{1,0:T(8,128)} %get-tuple-element.52.refs_0_, bf16[224,640]{1,0:T(8,128)(2,1)} %collective-permute-done.12.refs_1_, bf16[224,640]{1,0:T(8,128)(2,1)} %collective-permute-done.13.refs_2_, f32[640,224]{1,0:T(8,128)} %copy.14.refs_3_, ...), custom_call_target="tpu_custom_call" | custom-call | tf_op jit(solution)/shard_map/outer_step/pallas_call | solution.py:35
  201.4 2.9 %mix.1.refs_3_ = bf16[128,1792]{1,0:T(8,128)(2,1)} custom-call(s32[1]{0:T(128)} %bitcast.refs_0_, s32[2,128]{1,0:T(2,128)} %bitcast.23, f32[2,128]{1,0:T(2,128)} %bitcast.26, bf16[320,1792]{1,0:T(8,128)(2,1)} %bitcast.17, bf16[224,640]{1,0:T(8,128)(2,1)} %get-tuple-element.56.refs_4_.refs_1_), custom_call_target="tpu_custom_call" | custom-call | tf_op jit(solution)/shard_map/mix/pallas_call | solution.py:35
  206.0 2.7 %merge_in.1.refs_11_ = bf16[320,1792]{1,0:T(8,128)(2,1)} custom-call(bf16[160,1792]{1,0:T(8,128)(2,1)} %get-tuple-element.47.refs_2_.refs_0_, bf16[160,1792]{1,0:T(8,128)(2,1)} %copy-done.16, bf16[160,1792]{1,0:T(8,128)(2,1)} %copy-done.17, bf16[128,1792]{1,0:T(8,128)(2,1)} %mix.1.refs_3_), custom_call_target="tpu_custom_call" | custom-call | tf_op jit(solution)/shard_map/merge_in/pallas_call | solution.py:35
  208.6 6.3 %all-to-all-start.3 = ((bf16[8,40,1792]{2,1,0:T(8,128)(2,1)}), bf16[8,40,1792]{2,1,0:T(8,128)(2,1)S(1)}, u32[]{:S(2)}, u32[]{:S(2)}) async-start(bf16[8,40,1792]{2,1,0:T(8,128)(2,1)} %bitcast.14), calls=%async_computation.3 | async-start | bytes 2293760 | tf_op jit(solution)/shard_map/all_to_all | solution.py:265
  215.7 2.9 %collective-permute-start.17 = (bf16[224,640]{1,0:T(8,128)(2,1)S(1)}, bf16[224,640]{1,0:T(8,128)(2,1)S(1)}, u32[]{:S(2)}, u32[]{:S(2)}) collective-permute-start(bf16[224,640]{1,0:T(8,128)(2,1)S(1)} %copy-done.8), channel_id=1, source_target_pairs={{0,192},{32,224},{64,0},{96,32},{128,64},{160,96},{192,128},{224,1... | collective-permute-start | bytes 860168 | tf_op jit(solution)/shard_map/ppermute | solution.py:261
  218.6 5.7 %collective-permute-start.21 = (bf16[224,640]{1,0:T(8,128)(2,1)S(1)}, bf16[224,640]{1,0:T(8,128)(2,1)}, u32[]{:S(2)}, u32[]{:S(2)}) collective-permute-start(bf16[224,640]{1,0:T(8,128)(2,1)S(1)} %copy-done.8), channel_id=1, source_target_pairs={{0,32},{32,0},{64,96},{96,64},{128,160},{160,128},{192,224},{224,1... | collective-permute-start | bytes 860168 | tf_op jit(solution)/shard_map/ppermute | solution.py:261
  224.3 15.4 %collective-permute-done.18.refs_5_ = bf16[224,640]{1,0:T(8,128)(2,1)S(1)} collective-permute-done((bf16[224,640]{1,0:T(8,128)(2,1)S(1)}, bf16[224,640]{1,0:T(8,128)(2,1)S(1)}, u32[]{:S(2)}, u32[]{:S(2)}) %collective-permute-start.18) | collective-permute-done | bytes 286752 | tf_op jit(solution)/shard_map/ppermute | solution.py:261
  239.8 2.9 %collective-permute-start.19 = (bf16[112,640]{1,0:T(8,128)(2,1)S(1)}, bf16[112,640]{1,0:T(8,128)(2,1)S(1)}, u32[]{:S(2)}, u32[]{:S(2)}) collective-permute-start(bf16[112,640]{1,0:T(8,128)(2,1)S(1)} %slice.8), channel_id=1, source_target_pairs={{0,64},{32,96},{64,128},{96,160},{128,192},{160,224},{192,0},{224,... | collective-permute-start | bytes 430088 | tf_op jit(solution)/shard_map/ppermute | solution.py:261
  242.7 4.7 %collective-permute-start.22 = (bf16[224,640]{1,0:T(8,128)(2,1)S(1)}, bf16[224,640]{1,0:T(8,128)(2,1)}, u32[]{:S(2)}, u32[]{:S(2)}) collective-permute-start(bf16[224,640]{1,0:T(8,128)(2,1)S(1)} %collective-permute-done.17.refs_2_), channel_id=1, source_target_pairs={{0,32},{32,0},{64,96},{96,64},{128,160},{160,128},{192,224},{224,1... | collective-permute-start | bytes 860168 | tf_op jit(solution)/shard_map/ppermute | solution.py:261
  248.1 3.1 %collective-permute-start.23 = (bf16[112,640]{1,0:T(8,128)(2,1)S(1)}, bf16[112,640]{1,0:T(8,128)(2,1)}, u32[]{:S(2)}, u32[]{:S(2)}) collective-permute-start(bf16[112,640]{1,0:T(8,128)(2,1)S(1)} %collective-permute-done.19.refs_3_), channel_id=1, source_target_pairs={{0,32},{32,0},{64,96},{96,64},{128,160},{160,128},{192,224},{224,1... | collective-permute-start | bytes 430088 | tf_op jit(solution)/shard_map/ppermute | solution.py:261
  251.3 2.2 collective-permute-done.20.refs_4_
  256.8 4.0 %assemble.1.refs_3_ = bf16[640,1792]{1,0:T(8,128)(2,1)} custom-call(s32[2]{0:T(128)} %pad_add_fusion.refs_0_, bf16[224,640]{1,0:T(8,128)(2,1)} %get-tuple-element.56.refs_4_.refs_1_, bf16[224,640]{1,0:T(8,128)(2,1)} %copy-done.13, bf16[112,640]{1,0:T(8,128)(2,1)} %copy-done.27, bf16[112,640]{1,0:T(8,128)(2,1)} %collective-permute-done.20.refs_4_, ...), custom_call_target="tpu_custom_call" | custom-call | tf_op jit(solution)/shard_map/assemble/pallas_call | solution.py:35
  261.8 2.6 gather_grad.1
  (102 shorter events, 23.6 us)
Async XLA Ops:
  3.3 22.3 %all-to-all-start = ((bf16[8,40,1792]{2,1,0:T(8,128)(2,1)}), bf16[8,40,1792]{2,1,0:T(8,128)(2,1)S(1)}, u32[]{:S(2)}, u32[]{:S(2)}) async-start(bf16[8,40,1792]{2,1,0:T(8,128)(2,1)} %bitcast.15), calls=%async_computation | async-start | bytes 2293760 | tf_op jit(solution)/shard_map/all_to_all | solution.py:265
  26.6 18.7 %all-to-all-start.1 = ((bf16[8,40,1792]{2,1,0:T(8,128)(2,1)}), bf16[8,40,1792]{2,1,0:T(8,128)(2,1)S(1)}, u32[]{:S(2)}, u32[]{:S(2)}) async-start(bf16[8,40,1792]{2,1,0:T(8,128)(2,1)} %bitcast.20), calls=%async_computation.1 | async-start | bytes 2293760 | tf_op jit(solution)/shard_map/all_to_all | solution.py:265
  32.7 18.4 %copy-start.7 = (bf16[160,1792]{1,0:T(8,128)(2,1)S(1)}, bf16[160,1792]{1,0:T(8,128)(2,1)}, u32[]{:S(2)}) copy-start(bf16[160,1792]{1,0:T(8,128)(2,1)} %get-tuple-element.32.refs_1_.refs_0_) | copy-start | bytes 1720324
  32.7 18.4 %collective-permute-start = (bf16[160,1792]{1,0:T(8,128)(2,1)}, bf16[160,1792]{1,0:T(8,128)(2,1)S(1)}, u32[]{:S(2)}, u32[]{:S(2)}) collective-permute-start(bf16[160,1792]{1,0:T(8,128)(2,1)} %get-tuple-element.33), channel_id=1, source_target_pairs={{0,3},{1,2},{2,1},{3,0},{4,7},{5,6},{6,5},{7,4},{8,11},{9,10},{10,... | collective-permute-start | bytes 1720328 | tf_op jit(solution)/shard_map/ppermute | solution.py:258
  48.6 13.1 %collective-permute-start.6 = (bf16[160,1792]{1,0:T(8,128)(2,1)}, bf16[160,1792]{1,0:T(8,128)(2,1)S(1)}, u32[]{:S(2)}, u32[]{:S(2)}) collective-permute-start(bf16[160,1792]{1,0:T(8,128)(2,1)} %get-tuple-element.40), channel_id=1, source_target_pairs={{0,3},{1,2},{2,1},{3,0},{4,7},{5,6},{6,5},{7,4},{8,11},{9,10},{10,... | collective-permute-start | bytes 1720328 | tf_op jit(solution)/shard_map/ppermute | solution.py:258
  51.1 11.4 %collective-permute-start.1 = (bf16[160,1792]{1,0:T(8,128)(2,1)S(1)}, bf16[160,1792]{1,0:T(8,128)(2,1)S(1)}, u32[]{:S(2)}, u32[]{:S(2)}) collective-permute-start(bf16[160,1792]{1,0:T(8,128)(2,1)S(1)} %copy-done.7), channel_id=1, source_target_pairs={{0,1},{1,0},{2,3},{3,2},{4,5},{5,4},{6,7},{7,6},{8,9},{9,8},{10,11... | collective-permute-start | bytes 1720328 | tf_op jit(solution)/shard_map/ppermute | solution.py:255
  51.1 23.8 %copy-start.14 = (bf16[160,1792]{1,0:T(8,128)(2,1)}, bf16[160,1792]{1,0:T(8,128)(2,1)S(1)}, u32[]{:S(2)}) copy-start(bf16[160,1792]{1,0:T(8,128)(2,1)S(1)} %collective-permute-done.refs_1_) | copy-start | bytes 1720324
  51.1 23.8 %collective-permute-start.2 = (bf16[160,1792]{1,0:T(8,128)(2,1)S(1)}, bf16[160,1792]{1,0:T(8,128)(2,1)}, u32[]{:S(2)}, u32[]{:S(2)}) collective-permute-start(bf16[160,1792]{1,0:T(8,128)(2,1)S(1)} %collective-permute-done.refs_1_), channel_id=1, source_target_pairs={{0,1},{1,0},{2,3},{3,2},{4,5},{5,4},{6,7},{7,6},{8,9},{9,8},{10,11... | collective-permute-start | bytes 1720328 | tf_op jit(solution)/shard_map/ppermute | solution.py:255
  52.6 34.5 %collective-permute-start.3 = (bf16[160,1792]{1,0:T(8,128)(2,1)}, bf16[160,1792]{1,0:T(8,128)(2,1)S(1)}, u32[]{:S(2)}, u32[]{:S(2)}) collective-permute-start(bf16[160,1792]{1,0:T(8,128)(2,1)} %get-tuple-element.34.refs_6_.refs_1_.refs_0_), channel_id=1, source_target_pairs={{0,1},{1,0},{2,3},{3,2},{4,5},{5,4},{6,7},{7,6},{8,9},{9,8},{10,11... | collective-permute-start | bytes 1720328 | tf_op jit(solution)/shard_map/ppermute | solution.py:255
  61.7 22.0 %copy-start.5 = (bf16[160,1792]{1,0:T(8,128)(2,1)}, bf16[160,1792]{1,0:T(8,128)(2,1)S(1)}, u32[]{:S(2)}) copy-start(bf16[160,1792]{1,0:T(8,128)(2,1)S(1)} %collective-permute-done.6.refs_2_.refs_1_) | copy-start | bytes 1720324
  61.7 37.6 %collective-permute-start.7 = (bf16[160,1792]{1,0:T(8,128)(2,1)S(1)}, bf16[160,1792]{1,0:T(8,128)(2,1)S(1)}, u32[]{:S(2)}, u32[]{:S(2)}) collective-permute-start(bf16[160,1792]{1,0:T(8,128)(2,1)S(1)} %collective-permute-done.6.refs_2_.refs_1_), channel_id=1, source_target_pairs={{0,1},{1,0},{2,3},{3,2},{4,5},{5,4},{6,7},{7,6},{8,9},{9,8},{10,11... | collective-permute-start | bytes 1720328 | tf_op jit(solution)/shard_map/ppermute | solution.py:255
  62.6 12.3 %copy-start.15 = (bf16[160,1792]{1,0:T(8,128)(2,1)}, bf16[160,1792]{1,0:T(8,128)(2,1)S(1)}, u32[]{:S(2)}) copy-start(bf16[160,1792]{1,0:T(8,128)(2,1)S(1)} %collective-permute-done.1.refs_2_) | copy-start | bytes 1720324
  100.2 11.8 %copy-start.30 = (bf16[160,1792]{1,0:T(8,128)(2,1)S(1)}, bf16[160,1792]{1,0:T(8,128)(2,1)}, u32[]{:S(2)}) copy-start(bf16[160,1792]{1,0:T(8,128)(2,1)} %get-tuple-element.39) | copy-start | bytes 1720324
  100.2 11.8 %copy-start.29 = (bf16[160,1792]{1,0:T(8,128)(2,1)S(1)}, bf16[160,1792]{1,0:T(8,128)(2,1)}, u32[]{:S(2)}) copy-start(bf16[160,1792]{1,0:T(8,128)(2,1)} %get-tuple-element.37) | copy-start | bytes 1720324
  108.0 15.6 %collective-permute-start.8 = (bf16[896,640]{1,0:T(8,128)(2,1)}, bf16[896,640]{1,0:T(8,128)(2,1)S(1)}, u32[]{:S(2)}, u32[]{:S(2)}) collective-permute-start(bf16[896,640]{1,0:T(8,128)(2,1)} %get-tuple-element.44.refs_7_), channel_id=1, source_target_pairs={{0,32},{32,0},{64,96},{96,64},{128,160},{160,128},{192,224},{224,1... | collective-permute-start | bytes 3440648 | tf_op jit(solution)/shard_map/ppermute | solution.py:261
  112.0 25.8 %collective-permute-start.5 = (bf16[160,1792]{1,0:T(8,128)(2,1)S(1)}, bf16[160,1792]{1,0:T(8,128)(2,1)S(1)}, u32[]{:S(2)}, u32[]{:S(2)}) collective-permute-start(bf16[160,1792]{1,0:T(8,128)(2,1)S(1)} %copy-done.30), channel_id=1, source_target_pairs={{0,1},{1,0},{2,3},{3,2},{4,5},{5,4},{6,7},{7,6},{8,9},{9,8},{10,11... | collective-permute-start | bytes 1720328 | tf_op jit(solution)/shard_map/ppermute | solution.py:255
  112.0 45.0 %collective-permute-start.4 = (bf16[160,1792]{1,0:T(8,128)(2,1)S(1)}, bf16[160,1792]{1,0:T(8,128)(2,1)S(1)}, u32[]{:S(2)}, u32[]{:S(2)}) collective-permute-start(bf16[160,1792]{1,0:T(8,128)(2,1)S(1)} %copy-done.29), channel_id=1, source_target_pairs={{0,1},{1,0},{2,3},{3,2},{4,5},{5,4},{6,7},{7,6},{8,9},{9,8},{10,11... | collective-permute-start | bytes 1720328 | tf_op jit(solution)/shard_map/ppermute | solution.py:255
  138.6 2.4 copy-start.24
  138.6 5.4 %copy-start.31 = (bf16[112,640]{1,0:T(8,128)(2,1)S(1)}, bf16[112,640]{1,0:T(8,128)(2,1)}, u32[]{:S(2)}) copy-start(bf16[112,640]{1,0:T(8,128)(2,1)} %get-tuple-element.50) | copy-start | bytes 430084
  140.8 16.3 %collective-permute-start.9 = (bf16[160,1792]{1,0:T(8,128)(2,1)}, bf16[160,1792]{1,0:T(8,128)(2,1)S(1)}, u32[]{:S(2)}, u32[]{:S(2)}) collective-permute-start(bf16[160,1792]{1,0:T(8,128)(2,1)} %sum_out.1.refs_4_), channel_id=1, source_target_pairs={{0,3},{1,2},{2,1},{3,0},{4,7},{5,6},{6,5},{7,4},{8,11},{9,10},{10,... | collective-permute-start | bytes 1720328 | tf_op jit(solution)/shard_map/ppermute | solution.py:258
  141.0 9.2 %collective-permute-start.10 = (bf16[112,640]{1,0:T(8,128)(2,1)S(1)}, bf16[112,640]{1,0:T(8,128)(2,1)S(1)}, u32[]{:S(2)}, u32[]{:S(2)}) collective-permute-start(bf16[112,640]{1,0:T(8,128)(2,1)S(1)} %copy-done.24), channel_id=1, source_target_pairs={{0,64},{32,96},{64,128},{96,160},{128,192},{160,224},{192,0},{224,... | collective-permute-start | bytes 430088 | tf_op jit(solution)/shard_map/ppermute | solution.py:261
  144.0 10.3 %collective-permute-start.11 = (bf16[112,640]{1,0:T(8,128)(2,1)S(1)}, bf16[112,640]{1,0:T(8,128)(2,1)S(1)}, u32[]{:S(2)}, u32[]{:S(2)}) collective-permute-start(bf16[112,640]{1,0:T(8,128)(2,1)S(1)} %copy-done.31), channel_id=1, source_target_pairs={{0,192},{32,224},{64,0},{96,32},{128,64},{160,96},{192,128},{224,1... | collective-permute-start | bytes 430088 | tf_op jit(solution)/shard_map/ppermute | solution.py:261
  150.2 4.1 %copy-start.25 = (bf16[112,640]{1,0:T(8,128)(2,1)}, bf16[112,640]{1,0:T(8,128)(2,1)S(1)}, u32[]{:S(2)}) copy-start(bf16[112,640]{1,0:T(8,128)(2,1)S(1)} %collective-permute-done.10.refs_2_) | copy-start | bytes 430084
  160.7 3.7 %copy-start.28 = (bf16[160,1792]{1,0:T(8,128)(2,1)S(1)}, bf16[160,1792]{1,0:T(8,128)(2,1)}, u32[]{:S(2)}) copy-start(bf16[160,1792]{1,0:T(8,128)(2,1)} %get-tuple-element.55) | copy-start | bytes 1720324
  160.7 39.7 %all-to-all-start.2 = ((bf16[8,40,1792]{2,1,0:T(8,128)(2,1)}), bf16[8,40,1792]{2,1,0:T(8,128)(2,1)S(1)}, u32[]{:S(2)}, u32[]{:S(2)}) async-start(bf16[8,40,1792]{2,1,0:T(8,128)(2,1)} %bitcast.13), calls=%async_computation.2 | async-start | bytes 2293760 | tf_op jit(solution)/shard_map/all_to_all | solution.py:265
  164.4 12.8 %collective-permute-start.14 = (bf16[160,1792]{1,0:T(8,128)(2,1)S(1)}, bf16[160,1792]{1,0:T(8,128)(2,1)S(1)}, u32[]{:S(2)}, u32[]{:S(2)}) collective-permute-start(bf16[160,1792]{1,0:T(8,128)(2,1)S(1)} %copy-done.28), channel_id=1, source_target_pairs={{0,1},{1,0},{2,3},{3,2},{4,5},{5,4},{6,7},{7,6},{8,9},{9,8},{10,11... | collective-permute-start | bytes 1720328 | tf_op jit(solution)/shard_map/ppermute | solution.py:255
  164.5 39.8 %collective-permute-start.15 = (bf16[160,1792]{1,0:T(8,128)(2,1)}, bf16[160,1792]{1,0:T(8,128)(2,1)S(1)}, u32[]{:S(2)}, u32[]{:S(2)}) collective-permute-start(bf16[160,1792]{1,0:T(8,128)(2,1)} %get-tuple-element.45.refs_2_), channel_id=1, source_target_pairs={{0,1},{1,0},{2,3},{3,2},{4,5},{5,4},{6,7},{7,6},{8,9},{9,8},{10,11... | collective-permute-start | bytes 1720328 | tf_op jit(solution)/shard_map/ppermute | solution.py:255
  178.1 8.9 %copy-start.19 = (f32[640,224]{0,1:T(8,128)S(1)}, f32[640,224]{0,1:T(8,128)}, u32[]{:S(2)}) copy-start(f32[640,224]{0,1:T(8,128)} %param.16) | copy-start | bytes 1720324
  180.3 7.8 %copy-start.20 = (f32[640,224]{0,1:T(8,128)S(1)}, f32[640,224]{0,1:T(8,128)}, u32[]{:S(2)}) copy-start(f32[640,224]{0,1:T(8,128)} %param.17) | copy-start | bytes 1720324
  180.3 24.0 %collective-permute-start.16 = (bf16[160,1792]{1,0:T(8,128)(2,1)}, bf16[160,1792]{1,0:T(8,128)(2,1)S(1)}, u32[]{:S(2)}, u32[]{:S(2)}) collective-permute-start(bf16[160,1792]{1,0:T(8,128)(2,1)} %sum_in.1.refs_5_), channel_id=1, source_target_pairs={{0,3},{1,2},{2,1},{3,0},{4,7},{5,6},{6,5},{7,4},{8,11},{9,10},{10,... | collective-permute-start | bytes 1720328 | tf_op jit(solution)/shard_map/ppermute | solution.py:258
  182.8 14.0 %collective-permute-start.12 = (bf16[224,640]{1,0:T(8,128)(2,1)}, bf16[224,640]{1,0:T(8,128)(2,1)}, u32[]{:S(2)}, u32[]{:S(2)}) collective-permute-start(bf16[224,640]{1,0:T(8,128)(2,1)} %get-tuple-element.51.refs_3_), channel_id=1, source_target_pairs={{0,64},{32,96},{64,128},{96,160},{128,192},{160,224},{192,0},{224,... | collective-permute-start | bytes 860168 | tf_op jit(solution)/shard_map/ppermute | solution.py:261
  186.8 10.6 %collective-permute-start.13 = (bf16[224,640]{1,0:T(8,128)(2,1)}, bf16[224,640]{1,0:T(8,128)(2,1)}, u32[]{:S(2)}, u32[]{:S(2)}) collective-permute-start(bf16[224,640]{1,0:T(8,128)(2,1)} %get-tuple-element.53), channel_id=1, source_target_pairs={{0,192},{32,224},{64,0},{96,32},{128,64},{160,96},{192,128},{224,1... | collective-permute-start | bytes 860168 | tf_op jit(solution)/shard_map/ppermute | solution.py:261
  208.6 6.3 %copy-start.8 = (bf16[224,640]{1,0:T(8,128)(2,1)S(1)}, bf16[224,640]{1,0:T(8,128)(2,1)}, u32[]{:S(2)}) copy-start(bf16[224,640]{1,0:T(8,128)(2,1)} %get-tuple-element.56.refs_4_.refs_1_) | copy-start | bytes 860164
  208.6 46.0 %copy-start.11 = (f32[640,224]{1,0:T(8,128)S(1)}, f32[640,224]{1,0:T(8,128)}, u32[]{:S(2)}) copy-start(f32[640,224]{1,0:T(8,128)} %get-tuple-element.61) | copy-start | bytes 1720324
  208.6 52.1 %all-to-all-start.3 = ((bf16[8,40,1792]{2,1,0:T(8,128)(2,1)}), bf16[8,40,1792]{2,1,0:T(8,128)(2,1)S(1)}, u32[]{:S(2)}, u32[]{:S(2)}) async-start(bf16[8,40,1792]{2,1,0:T(8,128)(2,1)} %bitcast.14), calls=%async_computation.3 | async-start | bytes 2293760 | tf_op jit(solution)/shard_map/all_to_all | solution.py:265
  214.9 40.8 %copy-start.10 = (f32[640,224]{1,0:T(8,128)S(1)}, f32[640,224]{1,0:T(8,128)}, u32[]{:S(2)}) copy-start(f32[640,224]{1,0:T(8,128)} %get-tuple-element.62) | copy-start | bytes 1720324
  214.9 24.8 %collective-permute-start.18 = (bf16[224,640]{1,0:T(8,128)(2,1)S(1)}, bf16[224,640]{1,0:T(8,128)(2,1)S(1)}, u32[]{:S(2)}, u32[]{:S(2)}) collective-permute-start(bf16[224,640]{1,0:T(8,128)(2,1)S(1)} %copy-done.8), channel_id=1, source_target_pairs={{0,64},{32,96},{64,128},{96,160},{128,192},{160,224},{192,0},{224,... | collective-permute-start | bytes 860168 | tf_op jit(solution)/shard_map/ppermute | solution.py:261
  215.7 27.0 %collective-permute-start.17 = (bf16[224,640]{1,0:T(8,128)(2,1)S(1)}, bf16[224,640]{1,0:T(8,128)(2,1)S(1)}, u32[]{:S(2)}, u32[]{:S(2)}) collective-permute-start(bf16[224,640]{1,0:T(8,128)(2,1)S(1)} %copy-done.8), channel_id=1, source_target_pairs={{0,192},{32,224},{64,0},{96,32},{128,64},{160,96},{192,128},{224,1... | collective-permute-start | bytes 860168 | tf_op jit(solution)/shard_map/ppermute | solution.py:261
  218.6 38.2 %collective-permute-start.21 = (bf16[224,640]{1,0:T(8,128)(2,1)S(1)}, bf16[224,640]{1,0:T(8,128)(2,1)}, u32[]{:S(2)}, u32[]{:S(2)}) collective-permute-start(bf16[224,640]{1,0:T(8,128)(2,1)S(1)} %copy-done.8), channel_id=1, source_target_pairs={{0,32},{32,0},{64,96},{96,64},{128,160},{160,128},{192,224},{224,1... | collective-permute-start | bytes 860168 | tf_op jit(solution)/shard_map/ppermute | solution.py:261
  239.8 17.0 %copy-start.12 = (bf16[224,640]{1,0:T(8,128)(2,1)}, bf16[224,640]{1,0:T(8,128)(2,1)S(1)}, u32[]{:S(2)}) copy-start(bf16[224,640]{1,0:T(8,128)(2,1)S(1)} %collective-permute-done.18.refs_5_) | copy-start | bytes 860164
  239.8 8.3 %collective-permute-start.19 = (bf16[112,640]{1,0:T(8,128)(2,1)S(1)}, bf16[112,640]{1,0:T(8,128)(2,1)S(1)}, u32[]{:S(2)}, u32[]{:S(2)}) collective-permute-start(bf16[112,640]{1,0:T(8,128)(2,1)S(1)} %slice.8), channel_id=1, source_target_pairs={{0,64},{32,96},{64,128},{96,160},{128,192},{160,224},{192,0},{224,... | collective-permute-start | bytes 430088 | tf_op jit(solution)/shard_map/ppermute | solution.py:261
  242.7 14.1 %copy-start.13 = (bf16[224,640]{1,0:T(8,128)(2,1)}, bf16[224,640]{1,0:T(8,128)(2,1)S(1)}, u32[]{:S(2)}) copy-start(bf16[224,640]{1,0:T(8,128)(2,1)S(1)} %collective-permute-done.17.refs_2_) | copy-start | bytes 860164
  242.7 14.1 %collective-permute-start.22 = (bf16[224,640]{1,0:T(8,128)(2,1)S(1)}, bf16[224,640]{1,0:T(8,128)(2,1)}, u32[]{:S(2)}, u32[]{:S(2)}) collective-permute-start(bf16[224,640]{1,0:T(8,128)(2,1)S(1)} %collective-permute-done.17.refs_2_), channel_id=1, source_target_pairs={{0,32},{32,0},{64,96},{96,64},{128,160},{160,128},{192,224},{224,1... | collective-permute-start | bytes 860168 | tf_op jit(solution)/shard_map/ppermute | solution.py:261
  247.4 9.4 %collective-permute-start.25 = (bf16[224,640]{1,0:T(8,128)(2,1)S(1)}, bf16[224,640]{1,0:T(8,128)(2,1)}, u32[]{:S(2)}, u32[]{:S(2)}) collective-permute-start(bf16[224,640]{1,0:T(8,128)(2,1)S(1)} %collective-permute-done.18.refs_5_), channel_id=1, source_target_pairs={{0,32},{32,0},{64,96},{96,64},{128,160},{160,128},{192,224},{224,1... | collective-permute-start | bytes 860168 | tf_op jit(solution)/shard_map/ppermute | solution.py:261
  247.5 5.9 %collective-permute-start.20 = (bf16[112,640]{1,0:T(8,128)(2,1)S(1)}, bf16[112,640]{1,0:T(8,128)(2,1)}, u32[]{:S(2)}, u32[]{:S(2)}) collective-permute-start(bf16[112,640]{1,0:T(8,128)(2,1)S(1)} %slice.9), channel_id=1, source_target_pairs={{0,192},{32,224},{64,0},{96,32},{128,64},{160,96},{192,128},{224,1... | collective-permute-start | bytes 430088 | tf_op jit(solution)/shard_map/ppermute | solution.py:261
  248.1 8.7 %copy-start.27 = (bf16[112,640]{1,0:T(8,128)(2,1)}, bf16[112,640]{1,0:T(8,128)(2,1)S(1)}, u32[]{:S(2)}) copy-start(bf16[112,640]{1,0:T(8,128)(2,1)S(1)} %collective-permute-done.19.refs_3_) | copy-start | bytes 430084
  248.1 8.7 %collective-permute-start.23 = (bf16[112,640]{1,0:T(8,128)(2,1)S(1)}, bf16[112,640]{1,0:T(8,128)(2,1)}, u32[]{:S(2)}, u32[]{:S(2)}) collective-permute-start(bf16[112,640]{1,0:T(8,128)(2,1)S(1)} %collective-permute-done.19.refs_3_), channel_id=1, source_target_pairs={{0,32},{32,0},{64,96},{96,64},{128,160},{160,128},{192,224},{224,1... | collective-permute-start | bytes 430088 | tf_op jit(solution)/shard_map/ppermute | solution.py:261
  253.4 3.4 %collective-permute-start.24 = (bf16[112,640]{1,0:T(8,128)(2,1)}, bf16[112,640]{1,0:T(8,128)(2,1)}, u32[]{:S(2)}, u32[]{:S(2)}) collective-permute-start(bf16[112,640]{1,0:T(8,128)(2,1)} %collective-permute-done.20.refs_4_), channel_id=1, source_target_pairs={{0,32},{32,0},{64,96},{96,64},{128,160},{160,128},{192,224},{224,1... | collective-permute-start | bytes 430088 | tf_op jit(solution)/shard_map/ppermute | solution.py:261
  (14 other events, 12.4 us)
where the time goes:
time: 269 us; the launch traced here: 265 us
  waiting for transfers between devices  99.9 us (37%)
  Pallas kernels  78.9 us (29%)
  starting transfers between devices  68.2 us (25%)
  local copies, waits for them, and re-layouts  15.9 us (6%)
    pallas_call x19, Pallas kernels, call(): pl.pallas_call(body, out_shape=out_shape, in_specs=[SMEM] * smem + [VMEM]...  78.9 us
    ppermute x14, starting transfers between devices, by_z(): return lax.ppermute(v, 'island', perm)  35.5 us
    ppermute x14, waiting for transfers between devices, by_z(): return lax.ppermute(v, 'island', perm)  33.8 us
    ppermute x8, waiting for transfers between devices, to_pair(): return lax.ppermute(v, 'expert', pair)  33.8 us
    all_to_all x4, waiting for transfers between devices, exchange(): lax.all_to_all(v, 'expert', split_axis=0, concat_axis=0, tiled=True, axis...  23.3 us
    all_to_all x4, starting transfers between devices, exchange(): lax.all_to_all(v, 'expert', split_axis=0, concat_axis=0, tiled=True, axis...  20.1 us
    unnamed x68, local copies, waits for them, and re-layouts  15.9 us
    ppermute x4, waiting for transfers between devices, to_across(): return lax.ppermute(v, 'expert', across)  9.03 us
  transfers between devices with their start and end apart: 30, of which 13 were waited for; matrix products, arithmetic and copies ran while one was open for 2% of the time, Pallas kernels for 23%

commit v1 on v0

--- a/solution.py
+++ b/solution.py
@@ -25,7 +25,7 @@
 SMEM = pl.BlockSpec(memory_space=pltpu.SMEM)
 
 
-def call(kernel, out_shape, args, smem=0, after=(), scratch=(), name=None):
+def call(kernel, out_shape, args, smem=0, after=(), scratch=(), name=None, micros=0):
     args, after = list(args), list(after)
     count, skipped = len(args), len(after)
 
@@ -38,9 +38,14 @@
         in_specs=[SMEM] * smem + [VMEM] * (count - smem) + [pl.BlockSpec(memory_space=pl.ANY)] * skipped,
         out_specs=jax.tree.map(lambda _: VMEM, out_shape),
         scratch_shapes=scratch,
+        cost_estimate=pl.CostEstimate(flops=1_150_000_000 * micros, transcendentals=0, bytes_accessed=0),
         compiler_params=pltpu.CompilerParams(vmem_limit_bytes=60 * 1024 * 1024),
         name=name,
     )(*args, *after)
+
+
+def gate(value, *events):
+    return lax.optimization_barrier((value, *events))[0]
 
 
 def shape(rows, columns, dtype):
@@ -127,9 +132,11 @@
         out[...] = jnp.dot(block, down_ref[...], preferred_element_type=F32).astype(BF16)
 
 
-def backward(first, s0, s1, gate_ref, up_ref, down_ref, slope_ref, act_ref, o0, o1):
-    rows = s0.shape[0]
-    for c, (s, out) in enumerate(((s0, o0), (s1, o1))):
+def backward(first, *refs):
+    count = (len(refs) - 5) // 2
+    grads, (gate_ref, up_ref, down_ref, slope_ref, act_ref), outs = refs[:count], refs[count : count + 5], refs[count + 5 :]
+    rows = outs[0].shape[0]
+    for c, (s, out) in enumerate(zip(grads, outs)):
         chunk = pl.ds((first + c) * rows, rows)
         grad_hidden = lax.dot_general(s[...], down_ref[...], LAST, preferred_element_type=F32)
         grad_gate = (grad_hidden * slope_ref[chunk, :]).astype(BF16)
@@ -281,12 +288,15 @@
     )
     own_x, other_x = call(part(split_rows, capacity), (half_shape,) * 2, [exchange(packed_x)], name="split_x")
     crossed_x = to_across(other_x)
-    xs = (own_x, crossed_x, to_pair(own_x), to_pair(crossed_x))
+    near_x = to_pair(own_x)
+    far_x = to_pair(gate(crossed_x, near_x))
+    got_s = exchange(gate(packed_s, own_x))
     own_s, other_s = call(
-        part(split_rows, capacity), (half_shape,) * 2, [exchange(packed_s)], after=[own_x], name="split_s"
+        part(split_rows, capacity), (half_shape,) * 2, [gate(got_s, near_x, crossed_x)], name="split_s"
     )
     crossed_s = to_across(other_s)
-    ss = (own_s, crossed_s, to_pair(own_s), to_pair(crossed_s))
+    near_s = to_pair(own_s)
+    far_s = to_pair(gate(crossed_s, far_x))
 
     total_rows = 2 * slots
     hidden, slope, activated = call(
@@ -296,85 +306,98 @@
             shape(total_rows, hidden_count, F32),
             shape(total_rows, hidden_count, F32),
         ),
-        [*xs, w_gate, w_up],
-        after=[own_s],
+        [own_x, crossed_x, near_x, far_x, w_gate, w_up],
+        after=[own_s, crossed_s],
         name="forward",
     )
-    outs = call(down, (half_shape,) * 4, [hidden, w_down], after=[ss[2]], name="down")
+    outs = call(down, (half_shape,) * 4, [hidden, w_down], name="down")
+    far_out = to_pair(gate(outs[3], near_s))
+    near_out = to_pair(gate(outs[2], far_s))
 
     half_features = NZ * n
     mine, theirs = call(
         inner_step,
         (shape(half_features, hidden_count, F32), shape(half_features, hidden_count, BF16)),
-        [at, *ss, hidden, w_down],
+        [at, own_s, crossed_s, near_s, far_s, hidden, w_down],
         smem=1,
         after=[outs[0]],
         scratch=[pltpu.VMEM((features, hidden_count), F32)],
         name="inner_step",
+        micros=20,
     )
     from_core = by_z(theirs, other_core)
 
-    far_ins = call(
-        part(backward, 2),
-        (half_shape,) * 2,
-        [ss[2], ss[3], w_gate, w_up, w_down, slope, activated],
-        after=[theirs],
-        name="backward_far",
-    )
+    def back(first, grads, name, after):
+        return call(
+            part(backward, first),
+            (half_shape,) * len(grads),
+            [*grads, w_gate, w_up, w_down, slope, activated],
+            after=after,
+            name=name,
+            micros=20,
+        )
+
+    far_ins = back(2, [near_s, far_s], "backward_far", [theirs, far_out])
     block32, blockb, halfb = shape(n, hidden_count, F32), shape(n, hidden_count, BF16), shape(h, hidden_count, BF16)
     own_sum, before, after, far_low, far_high = call(
-        core_sum, (block32,) * 3 + (halfb,) * 2, [mine, from_core], after=[far_ins[0]], name="core_sum"
-    )
-    near_ins = call(
-        part(backward, 0),
-        (half_shape,) * 2,
-        [ss[0], ss[1], w_gate, w_up, w_down, slope, activated],
-        after=[far_low],
-        name="backward_near",
-    )
-
-    sum_out = call(add_rows, half_shape, [outs[1], to_pair(outs[3])], after=[near_ins[0]], name="sum_out")
+        core_sum, (block32,) * 3 + (halfb,) * 2, [mine, from_core], after=[far_ins[0]], name="core_sum", micros=3
+    )
+
+    sum_out = call(add_rows, half_shape, [outs[1], far_out], after=[far_low, near_out], name="sum_out", micros=2)
+    across_out = to_across(sum_out)
+    far_in = to_pair(gate(far_ins[1], far_out))
+    (crossed_in,) = back(1, [crossed_s], "backward_crossed", [sum_out])
     to_next, to_last = call(
         ring_sum,
         (blockb,) * 2,
         [before, after, by_z(far_low, ahead), by_z(far_high, behind)],
-        after=[sum_out],
+        after=[crossed_in],
         name="ring_sum",
-    )
+        micros=2,
+    )
+    from_left, from_right = by_z(to_next, ahead), by_z(to_last, behind)
+    sum_in = call(add_rows, half_shape, [crossed_in, far_in], after=[to_next], name="sum_in", micros=2)
+    across_in = to_across(sum_in)
+    near_in = to_pair(gate(far_ins[0], near_out))
+    (own_in,) = back(0, [own_s], "backward_own", [sum_in])
     merged_out = call(
         part(merge_rows, capacity),
         whole_shape,
-        [outs[0], to_pair(outs[2]), to_across(sum_out)],
-        after=[to_next],
+        [outs[0], near_out, across_out],
+        after=[own_in],
         name="merge_out",
-    )
-    sum_in = call(add_rows, half_shape, [near_ins[1], to_pair(far_ins[1])], after=[merged_out], name="sum_in")
+        micros=0,
+    )
+    back_out = exchange(merged_out)
     outer_next, momentum_next, fresh = call(
         part(outer_step, islands),
         (shape(hidden_count, n, F32), shape(hidden_count, n, F32), blockb),
-        [own_sum, by_z(to_next, ahead), by_z(to_last, behind), outer_down, momentum],
-        after=[sum_in],
+        [own_sum, from_left, from_right, outer_down, momentum],
+        after=[merged_out, near_in],
         name="outer_step",
-    )
+        micros=3,
+    )
+    left, right = by_z(fresh, ahead), by_z(fresh, behind)
+    merged_in = call(
+        part(merge_rows, capacity),
+        whole_shape,
+        [own_in, near_in, across_in],
+        after=[fresh],
+        name="merge_in",
+        micros=16,
+    )
+    back_in = exchange(merged_in)
     mixed = call(
         part(mix, capacity),
         shape(token_count, features, BF16),
-        [xp, routes, weights, exchange(merged_out)],
+        [xp, routes, weights, back_out],
         smem=1,
-        after=[fresh],
+        after=[merged_in],
         name="mix",
-    )
-    merged_in = call(
-        part(merge_rows, capacity),
-        whole_shape,
-        [near_ins[0], to_pair(far_ins[0]), to_across(sum_in)],
-        after=[mixed],
-        name="merge_in",
-    )
-    left = by_z(fresh, ahead)
-    right = by_z(fresh, behind)
-    low = by_z(left[:h], ahead)
-    high = by_z(right[h:], behind)
+        micros=0,
+    )
+    left, right = gate(left, mixed), gate(right, mixed)
+    low, high = by_z(left[:h], ahead), by_z(right[h:], behind)
     blocks = [fresh, right, low, high, left]
     blocks += [by_z(b, other_core) for b in blocks]
     fresh_down = call(
@@ -382,17 +405,19 @@
         shape(hidden_count, features, BF16),
         [at, *blocks],
         smem=1,
-        after=[merged_in],
+        after=[mixed],
         scratch=[pltpu.VMEM((features, hidden_count), F32)],
         name="assemble",
+        micros=14,
     )
     input_grad = call(
         part(gather_grad, capacity),
         shape(token_count, features, BF16),
-        [xp, routes, exchange(merged_in)],
+        [xp, routes, back_in],
         smem=1,
         after=[fresh_down],
         name="gather_grad",
+        micros=3,
     )
     return mixed, input_grad, outer_next, momentum_next, fresh_down
 

time: 269 us -> 233 us (0.87)
  waiting for transfers between devices: 99.9 us -> 49.3 us
  starting transfers between devices: 68.2 us -> 78.8 us
  Pallas kernels: 78.9 us -> 84 us
    ppermute x14, waiting for transfers between devices: 33.8 us -> 6.3 us  [by_z(): return lax.ppermute(v, 'island', perm)]
    ppermute x8, waiting for transfers between devices: 33.8 us -> 7.28 us  [to_pair(): return lax.ppermute(v, 'expert', pair)]
    ppermute x14, starting transfers between devices: 35.5 us -> 49.1 us  [by_z(): return lax.ppermute(v, 'island', perm)]
    ppermute x4, waiting for transfers between devices: 9.03 us -> 17.5 us  [to_across(): return lax.ppermute(v, 'expert', across)]
    pallas_call x19 -> x20, Pallas kernels: 78.9 us -> 84 us  [call(): pl.pallas_call(body, out_shape=out_shape, in_specs=[SMEM] * smem + [VMEM]...]
    all_to_all x4, waiting for transfers between devices: 23.3 us -> 18.2 us  [exchange(): lax.all_to_all(v, 'expert', split_axis=0, concat_axis=0, tiled=True, axis...]
    unnamed x68 -> x64, local copies, waits for them, and re-layouts: 15.9 us -> 15 us
  transfers between devices with their start and end apart: 30 -> 30, of which waited for: 13 -> 8; matrix products, arithmetic and copies ran while one was open for 2% -> 2% of each run, Pallas kernels for 23% -> 33%
where the time goes in v1:
time: 233 us; the launch traced here: 229 us
  Pallas kernels  84 us (36%)
  starting transfers between devices  78.8 us (34%)
  waiting for transfers between devices  49.3 us (21%)
  local copies, waits for them, and re-layouts  15.1 us (6%)
    pallas_call x20, Pallas kernels, call(): pl.pallas_call(body, out_shape=out_shape, in_specs=[SMEM] * smem + [VMEM]...  84 us
    ppermute x14, starting transfers between devices, by_z(): return lax.ppermute(v, 'island', perm)  49.1 us
    all_to_all x4, starting transfers between devices, exchange(): lax.all_to_all(v, 'expert', split_axis=0, concat_axis=0, tiled=True, axis...  18.9 us
    all_to_all x4, waiting for transfers between devices, exchange(): lax.all_to_all(v, 'expert', split_axis=0, concat_axis=0, tiled=True, axis...  18.2 us
    ppermute x4, waiting for transfers between devices, to_across(): return lax.ppermute(v, 'expert', across)  17.5 us
    unnamed x64, local copies, waits for them, and re-layouts  15 us
    ppermute x8, waiting for transfers between devices, to_pair(): return lax.ppermute(v, 'expert', pair)  7.28 us
    ppermute x4, starting transfers between devices, to_across(): return lax.ppermute(v, 'expert', across)  6.97 us
  transfers between devices with their start and end apart: 30, of which 8 were waited for; matrix products, arithmetic and copies ran while one was open for 2% of the time, Pallas kernels for 33%

profile of v1, /device:TPU:1, one launch (start us, length us, event | category | flops | bytes accessed | tf_op | source)
XLA Modules:
  0.0 228.8 jit_solution(9160817162191201140)
XLA Ops:
  0.7 2.6 %pack_tokens.1.refs_4_ = bf16[320,1792]{1,0:T(8,128)(2,1)} custom-call(s32[1]{0:T(128)} %bitcast.refs_0_, s32[2,128]{1,0:T(2,128)} %bitcast.20, bf16[128,1792]{1,0:T(8,128)(2,1)} %refs_2_.4), custom_call_target="tpu_custom_call" | custom-call | tf_op jit(solution)/shard_map/pack_tokens/pallas_call | solution.py:35
  3.3 6.4 %all-to-all-start = ((bf16[8,40,1792]{2,1,0:T(8,128)(2,1)}), bf16[8,40,1792]{2,1,0:T(8,128)(2,1)S(1)}, u32[]{:S(2)}, u32[]{:S(2)}) async-start(bf16[8,40,1792]{2,1,0:T(8,128)(2,1)} %bitcast.13), calls=%async_computation | async-start | bytes 2293760 | tf_op jit(solution)/shard_map/all_to_all | solution.py:272
  9.7 2.7 %pack_scores.1 = bf16[320,1792]{1,0:T(8,128)(2,1)} custom-call(s32[1]{0:T(128)} %bitcast.refs_0_, s32[2,128]{1,0:T(2,128)} %bitcast.21, f32[2,128]{1,0:T(2,128)} %bitcast.24, bf16[128,1792]{1,0:T(8,128)(2,1)} %refs_3_.5, bf16[320,1792]{1,0:T(8,128)(2,1)} %pack_tokens.1.refs_4_), custom_call_target="tpu_custom_call" | custom-call | tf_op jit(solution)/shard_map/pack_scores/pallas_call | solution.py:35
  12.4 13.2 %all-to-all-done = bf16[8,40,1792]{2,1,0:T(8,128)(2,1)S(1)} async-done(((bf16[8,40,1792]{2,1,0:T(8,128)(2,1)}), bf16[8,40,1792]{2,1,0:T(8,128)(2,1)S(1)}, u32[]{:S(2)}, u32[]{:S(2)}) %all-to-all-start) | async-done | bytes 1146912 | tf_op jit(solution)/shard_map/all_to_all | solution.py:272
  26.6 2.4 %split_x.1 = (bf16[160,1792]{1,0:T(8,128)(2,1)}, bf16[160,1792]{1,0:T(8,128)(2,1)}) custom-call(bf16[320,1792]{1,0:T(8,128)(2,1)} %bitcast.15), custom_call_target="tpu_custom_call" | custom-call | tf_op jit(solution)/shard_map/split_x/pallas_call | solution.py:35
  28.9 3.9 %all-to-all-start.1 = ((bf16[8,40,1792]{2,1,0:T(8,128)(2,1)}), bf16[8,40,1792]{2,1,0:T(8,128)(2,1)S(1)}, u32[]{:S(2)}, u32[]{:S(2)}) async-start(bf16[8,40,1792]{2,1,0:T(8,128)(2,1)} %bitcast.5), calls=%async_computation.1 | async-start | bytes 2293760 | tf_op jit(solution)/shard_map/all_to_all | solution.py:272
  32.8 2.6 %collective-permute-start = (bf16[160,1792]{1,0:T(8,128)(2,1)}, bf16[160,1792]{1,0:T(8,128)(2,1)S(1)}, u32[]{:S(2)}, u32[]{:S(2)}) collective-permute-start(bf16[160,1792]{1,0:T(8,128)(2,1)} %get-tuple-element.41), channel_id=1, source_target_pairs={{0,3},{1,2},{2,1},{3,0},{4,7},{5,6},{6,5},{7,4},{8,11},{9,10},{10,... | collective-permute-start | bytes 1720328 | tf_op jit(solution)/shard_map/ppermute | solution.py:265
  35.4 11.7 %collective-permute-done.refs_1_ = bf16[160,1792]{1,0:T(8,128)(2,1)S(1)} collective-permute-done((bf16[160,1792]{1,0:T(8,128)(2,1)}, bf16[160,1792]{1,0:T(8,128)(2,1)S(1)}, u32[]{:S(2)}, u32[]{:S(2)}) %collective-permute-start) | collective-permute-done | bytes 573472 | tf_op jit(solution)/shard_map/ppermute | solution.py:265
  49.8 2.5 %split_s.1 = (bf16[160,1792]{1,0:T(8,128)(2,1)}, bf16[160,1792]{1,0:T(8,128)(2,1)}) custom-call(bf16[320,1792]{1,0:T(8,128)(2,1)} %bitcast.14), custom_call_target="tpu_custom_call" | custom-call | tf_op jit(solution)/shard_map/split_s/pallas_call | solution.py:35
  52.2 1.7 collective-permute-start.3
  54.1 5.5 %collective-permute-done.2.refs_3_ = bf16[160,1792]{1,0:T(8,128)(2,1)S(1)} collective-permute-done((bf16[160,1792]{1,0:T(8,128)(2,1)S(1)}, bf16[160,1792]{1,0:T(8,128)(2,1)S(1)}, u32[]{:S(2)}, u32[]{:S(2)}) %collective-permute-start.2) | collective-permute-done | bytes 573472 | tf_op jit(solution)/shard_map/ppermute | solution.py:262
  59.6 5.7 %collective-permute-done.3.refs_7_.refs_2_.refs_0_ = bf16[160,1792]{1,0:T(8,128)(2,1)S(1)} collective-permute-done((bf16[160,1792]{1,0:T(8,128)(2,1)}, bf16[160,1792]{1,0:T(8,128)(2,1)S(1)}, u32[]{:S(2)}, u32[]{:S(2)}) %collective-permute-start.3) | collective-permute-done | bytes 573472 | tf_op jit(solution)/shard_map/ppermute | solution.py:265
  65.3 1.1 copy.14.refs_3_
  68.1 9.0 %forward.1 = (bf16[640,640]{1,0:T(8,128)(2,1)}, f32[640,640]{1,0:T(8,128)}, f32[640,640]{1,0:T(8,128)}) custom-call(bf16[160,1792]{1,0:T(8,128)(2,1)} %get-tuple-element.40.refs_0_, bf16[160,1792]{1,0:T(8,128)(2,1)} %copy-done.12, bf16[160,1792]{1,0:T(8,128)(2,1)} %copy-done.13, bf16[160,1792]{1,0:T(8,128)(2,1)} %copy-done.14, bf16[1792,640]{1,0:T(8,128)(2,1)} %refs_1_.5, ...), custom_call_target="tpu_custom_call" | custom-call | tf_op jit(solution)/shard_map/forward/pallas_call | solution.py:35
  77.1 4.7 %down.1 = (bf16[160,1792]{1,0:T(8,128)(2,1)}, bf16[160,1792]{1,0:T(8,128)(2,1)}, bf16[160,1792]{1,0:T(8,128)(2,1)}, bf16[160,1792]{1,0:T(8,128)(2,1)}) custom-call(bf16[640,640]{1,0:T(8,128)(2,1)} %get-tuple-element.47.refs_0_.refs_5_, bf16[640,1792]{1,0:T(8,128)(2,1)} %refs_3_.8), custom_call_target="tpu_custom_call" | custom-call | tf_op jit(solution)/shard_map/down/pallas_call | solution.py:35
  81.8 1.5 collective-permute-start.7
  84.6 7.7 %inner_step.1 = (f32[896,640]{1,0:T(8,128)}, bf16[896,640]{1,0:T(8,128)(2,1)}) custom-call(s32[2]{0:T(128)} %pad_add_fusion.refs_0_, bf16[160,1792]{1,0:T(8,128)(2,1)} %get-tuple-element.45.refs_6_.refs_1_.refs_0_, bf16[160,1792]{1,0:T(8,128)(2,1)} %copy-done.10, bf16[160,1792]{1,0:T(8,128)(2,1)} %copy-done.19, ...), custom_call_target="tpu_custom_call" | custom-call | flops 23000000512 | tf_op jit(solution)/shard_map/inner_step/pallas_call | solution.py:35
  92.3 6.5 %collective-permute-start.8 = (bf16[896,640]{1,0:T(8,128)(2,1)}, bf16[896,640]{1,0:T(8,128)(2,1)S(1)}, u32[]{:S(2)}, u32[]{:S(2)}) collective-permute-start(bf16[896,640]{1,0:T(8,128)(2,1)} %get-tuple-element.56.refs_7_), channel_id=1, source_target_pairs={{0,32},{32,0},{64,96},{96,64},{128,160},{160,128},{192,224},{224,1... | collective-permute-start | bytes 3440648 | tf_op jit(solution)/shard_map/ppermute | solution.py:268
  99.6 9.9 %backward_far.1 = (bf16[160,1792]{1,0:T(8,128)(2,1)}, bf16[160,1792]{1,0:T(8,128)(2,1)}) custom-call(bf16[160,1792]{1,0:T(8,128)(2,1)} %copy-done.19, bf16[160,1792]{1,0:T(8,128)(2,1)} %collective-permute-done.4.refs_4_.refs_1_, bf16[1792,640]{1,0:T(8,128)(2,1)} %refs_1_.5, bf16[1792,640]{1,0:T(8,128)(2,1)} %refs_2_.7, bf16[640,1792]{1,0:T(8,128)(2,1)} %refs_3_.8, ...), custom_call_target="tpu_custom_call" | custom-call | flops 23000000512 | tf_op jit(solution)/shard_map/backward_far/pallas_call | solution.py:35
  109.5 1.7 collective-permute-start.10
  112.4 3.3 %core_sum.1 = (f32[224,640]{1,0:T(8,128)}, f32[224,640]{1,0:T(8,128)}, f32[224,640]{1,0:T(8,128)}, bf16[112,640]{1,0:T(8,128)(2,1)}, bf16[112,640]{1,0:T(8,128)(2,1)}) custom-call(f32[896,640]{1,0:T(8,128)} %get-tuple-element.55.refs_0_, bf16[896,640]{1,0:T(8,128)(2,1)} %copy-done.17, bf16[160,1792]{1,0:T(8,128)(2,1)} %get-tuple-element.67.refs_2_), custom_call_target="tpu_custom_call" | custom-call | flops 3449999872 | tf_op jit(solution)/shard_map/core_sum/pallas_call | solution.py:35
  115.7 3.0 %collective-permute-start.11 = (bf16[112,640]{1,0:T(8,128)(2,1)}, bf16[112,640]{1,0:T(8,128)(2,1)S(1)}, u32[]{:S(2)}, u32[]{:S(2)}) collective-permute-start(bf16[112,640]{1,0:T(8,128)(2,1)} %get-tuple-element.60.refs_2_), channel_id=1, source_target_pairs={{0,64},{32,96},{64,128},{96,160},{128,192},{160,224},{192,0},{224,... | collective-permute-start | bytes 430088 | tf_op jit(solution)/shard_map/ppermute | solution.py:268
  118.7 2.2 sum_out.1.refs_6_
  120.9 1.6 collective-permute-start.9
  122.5 12.2 %collective-permute-start.12 = (bf16[112,640]{1,0:T(8,128)(2,1)S(1)}, bf16[112,640]{1,0:T(8,128)(2,1)S(1)}, u32[]{:S(2)}, u32[]{:S(2)}) collective-permute-start(bf16[112,640]{1,0:T(8,128)(2,1)S(1)} %copy-done.27), channel_id=1, source_target_pairs={{0,192},{32,224},{64,0},{96,32},{128,64},{160,96},{192,128},{224,1... | collective-permute-start | bytes 430088 | tf_op jit(solution)/shard_map/ppermute | solution.py:268
  134.7 7.4 %backward_crossed.1.refs_4_.refs_0_ = bf16[160,1792]{1,0:T(8,128)(2,1)} custom-call(bf16[160,1792]{1,0:T(8,128)(2,1)} %copy-done.10, bf16[1792,640]{1,0:T(8,128)(2,1)} %refs_1_.5, bf16[1792,640]{1,0:T(8,128)(2,1)} %refs_2_.7, bf16[640,1792]{1,0:T(8,128)(2,1)} %refs_3_.8, f32[640,640]{1,0:T(8,128)} %get-tuple-element.57.refs_5_.refs_4_, ...), custom_call_target="tpu_custom_call" | custom-call | flops 23000000512 | tf_op jit(solution)/shard_map/backward_crossed/pallas_call | solution.py:35
  142.8 2.1 ring_sum.1
  144.9 1.4 collective-permute-start.15
  147.2 2.2 sum_in.1.refs_6_
  149.4 1.1 collective-permute-start.14
  150.5 2.2 collective-permute-start.16
  152.6 7.4 %backward_own.1.refs_3_.refs_0_ = bf16[160,1792]{1,0:T(8,128)(2,1)} custom-call(bf16[160,1792]{1,0:T(8,128)(2,1)} %get-tuple-element.45.refs_6_.refs_1_.refs_0_, bf16[1792,640]{1,0:T(8,128)(2,1)} %refs_1_.5, bf16[1792,640]{1,0:T(8,128)(2,1)} %refs_2_.7, bf16[640,1792]{1,0:T(8,128)(2,1)} %refs_3_.8, f32[640,640]{1,0:T(8,128)} %get-tuple-element.57.refs_5_.refs_4_, ...), custom_call_target="tpu_custom_call" | custom-call | flops 23000000512 | tf_op jit(solution)/shard_map/backward_own/pallas_call | solution.py:35
  160.9 2.6 %merge_out.1.refs_5_ = bf16[320,1792]{1,0:T(8,128)(2,1)} custom-call(bf16[160,1792]{1,0:T(8,128)(2,1)} %get-tuple-element.48.refs_7_.refs_0_, bf16[160,1792]{1,0:T(8,128)(2,1)} %copy-done.6, bf16[160,1792]{1,0:T(8,128)(2,1)} %copy-done.7, bf16[160,1792]{1,0:T(8,128)(2,1)} %backward_own.1.refs_3_.refs_0_), custom_call_target="tpu_custom_call" | custom-call | tf_op jit(solution)/shard_map/merge_out/pallas_call | solution.py:35
  163.5 5.1 %all-to-all-start.2 = ((bf16[8,40,1792]{2,1,0:T(8,128)(2,1)}), bf16[8,40,1792]{2,1,0:T(8,128)(2,1)S(1)}, u32[]{:S(2)}, u32[]{:S(2)}) async-start(bf16[8,40,1792]{2,1,0:T(8,128)(2,1)} %bitcast.18), calls=%async_computation.2 | async-start | bytes 2293760 | tf_op jit(solution)/shard_map/all_to_all | solution.py:272
  169.5 3.1 %outer_step.1 = (f32[640,224]{1,0:T(8,128)}, f32[640,224]{1,0:T(8,128)}, bf16[224,640]{1,0:T(8,128)(2,1)}) custom-call(f32[224,640]{1,0:T(8,128)} %get-tuple-element.68.refs_0_, bf16[224,640]{1,0:T(8,128)(2,1)} %copy-done.24, bf16[224,640]{1,0:T(8,128)(2,1)} %collective-permute-done.16.refs_2_, f32[640,224]{1,0:T(8,128)} %copy.14.refs_3_, ...), custom_call_target="tpu_custom_call" | custom-call | flops 3449999872 | tf_op jit(solution)/shard_map/outer_step/pallas_call | solution.py:35
  172.6 1.2 collective-permute-start.17
  173.7 1.2 collective-permute-start.18
  175.7 2.7 %merge_in.1.refs_4_ = bf16[320,1792]{1,0:T(8,128)(2,1)} custom-call(bf16[160,1792]{1,0:T(8,128)(2,1)} %backward_own.1.refs_3_.refs_0_, bf16[160,1792]{1,0:T(8,128)(2,1)} %copy-done.18, bf16[160,1792]{1,0:T(8,128)(2,1)} %copy-done.22, bf16[224,640]{1,0:T(8,128)(2,1)} %get-tuple-element.70.refs_3_.refs_1_), custom_call_target="tpu_custom_call" | custom-call | flops 18400000000 | tf_op jit(solution)/shard_map/merge_in/pallas_call | solution.py:35
  178.4 5.1 %all-to-all-done.2 = bf16[8,40,1792]{2,1,0:T(8,128)(2,1)S(1)} async-done(((bf16[8,40,1792]{2,1,0:T(8,128)(2,1)}), bf16[8,40,1792]{2,1,0:T(8,128)(2,1)S(1)}, u32[]{:S(2)}, u32[]{:S(2)}) %all-to-all-start.2) | async-done | bytes 1146912 | tf_op jit(solution)/shard_map/all_to_all | solution.py:272
  184.5 3.6 %all-to-all-start.3 = ((bf16[8,40,1792]{2,1,0:T(8,128)(2,1)}), bf16[8,40,1792]{2,1,0:T(8,128)(2,1)S(1)}, u32[]{:S(2)}, u32[]{:S(2)}) async-start(bf16[8,40,1792]{2,1,0:T(8,128)(2,1)} %bitcast.16), calls=%async_computation.3 | async-start | bytes 2293760 | tf_op jit(solution)/shard_map/all_to_all | solution.py:272
  188.1 14.3 %collective-permute-start.21 = (bf16[224,640]{1,0:T(8,128)(2,1)S(1)}, bf16[224,640]{1,0:T(8,128)(2,1)}, u32[]{:S(2)}, u32[]{:S(2)}) collective-permute-start(bf16[224,640]{1,0:T(8,128)(2,1)S(1)} %copy-done.23), channel_id=1, source_target_pairs={{0,32},{32,0},{64,96},{96,64},{128,160},{160,128},{192,224},{224,1... | collective-permute-start | bytes 860168 | tf_op jit(solution)/shard_map/ppermute | solution.py:268
  202.3 3.0 %mix.1.refs_11_ = bf16[128,1792]{1,0:T(8,128)(2,1)} custom-call(s32[1]{0:T(128)} %bitcast.refs_0_, s32[2,128]{1,0:T(2,128)} %bitcast.22, f32[2,128]{1,0:T(2,128)} %bitcast.25, bf16[320,1792]{1,0:T(8,128)(2,1)} %bitcast.17, bf16[320,1792]{1,0:T(8,128)(2,1)} %merge_in.1.refs_4_), custom_call_target="tpu_custom_call" | custom-call | tf_op jit(solution)/shard_map/mix/pallas_call | solution.py:35
  205.4 2.5 %collective-permute-start.19 = (bf16[112,640]{1,0:T(8,128)(2,1)S(1)}, bf16[112,640]{1,0:T(8,128)(2,1)S(1)}, u32[]{:S(2)}, u32[]{:S(2)}) collective-permute-start(bf16[112,640]{1,0:T(8,128)(2,1)S(1)} %slice.6), channel_id=1, source_target_pairs={{0,64},{32,96},{64,128},{96,160},{128,192},{160,224},{192,0},{224,... | collective-permute-start | bytes 430088 | tf_op jit(solution)/shard_map/ppermute | solution.py:268
  208.2 1.2 collective-permute-start.20
  209.9 6.3 %collective-permute-done.19.refs_3_ = bf16[112,640]{1,0:T(8,128)(2,1)S(1)} collective-permute-done((bf16[112,640]{1,0:T(8,128)(2,1)S(1)}, bf16[112,640]{1,0:T(8,128)(2,1)S(1)}, u32[]{:S(2)}, u32[]{:S(2)}) %collective-permute-start.19) | collective-permute-done | bytes 143392 | tf_op jit(solution)/shard_map/ppermute | solution.py:268
  216.2 2.6 %collective-permute-start.23 = (bf16[112,640]{1,0:T(8,128)(2,1)S(1)}, bf16[112,640]{1,0:T(8,128)(2,1)}, u32[]{:S(2)}, u32[]{:S(2)}) collective-permute-start(bf16[112,640]{1,0:T(8,128)(2,1)S(1)} %collective-permute-done.19.refs_3_), channel_id=1, source_target_pairs={{0,32},{32,0},{64,96},{96,64},{128,160},{160,128},{192,224},{224,1... | collective-permute-start | bytes 430088 | tf_op jit(solution)/shard_map/ppermute | solution.py:268
  221.0 4.0 %assemble.1.refs_3_ = bf16[640,1792]{1,0:T(8,128)(2,1)} custom-call(s32[2]{0:T(128)} %pad_add_fusion.refs_0_, bf16[224,640]{1,0:T(8,128)(2,1)} %get-tuple-element.70.refs_3_.refs_1_, bf16[224,640]{1,0:T(8,128)(2,1)} %copy-done.15, bf16[112,640]{1,0:T(8,128)(2,1)} %copy-done.26, bf16[112,640]{1,0:T(8,128)(2,1)} %collective-permute-done.20.refs_4_, ...), custom_call_target="tpu_custom_call" | custom-call | flops 16099999744 | tf_op jit(solution)/shard_map/assemble/pallas_call | solution.py:35
  226.0 2.6 %gather_grad.1 = bf16[128,1792]{1,0:T(8,128)(2,1)} custom-call(s32[1]{0:T(128)} %bitcast.refs_0_, s32[2,128]{1,0:T(2,128)} %bitcast.23, bf16[320,1792]{1,0:T(8,128)(2,1)} %bitcast.19, bf16[640,1792]{1,0:T(8,128)(2,1)} %assemble.1.refs_3_), custom_call_target="tpu_custom_call" | custom-call | flops 3449999872 | tf_op jit(solution)/shard_map/gather_grad/pallas_call | solution.py:35
  (99 shorter events, 17.9 us)
Async XLA Ops:
  3.3 22.3 %all-to-all-start = ((bf16[8,40,1792]{2,1,0:T(8,128)(2,1)}), bf16[8,40,1792]{2,1,0:T(8,128)(2,1)S(1)}, u32[]{:S(2)}, u32[]{:S(2)}) async-start(bf16[8,40,1792]{2,1,0:T(8,128)(2,1)} %bitcast.13), calls=%async_computation | async-start | bytes 2293760 | tf_op jit(solution)/shard_map/all_to_all | solution.py:272
  28.9 6.5 %copy-start.11 = (bf16[160,1792]{1,0:T(8,128)(2,1)S(1)}, bf16[160,1792]{1,0:T(8,128)(2,1)}, u32[]{:S(2)}) copy-start(bf16[160,1792]{1,0:T(8,128)(2,1)} %get-tuple-element.40.refs_0_) | copy-start | bytes 1720324
  28.9 19.1 %all-to-all-start.1 = ((bf16[8,40,1792]{2,1,0:T(8,128)(2,1)}), bf16[8,40,1792]{2,1,0:T(8,128)(2,1)S(1)}, u32[]{:S(2)}, u32[]{:S(2)}) async-start(bf16[8,40,1792]{2,1,0:T(8,128)(2,1)} %bitcast.5), calls=%async_computation.1 | async-start | bytes 2293760 | tf_op jit(solution)/shard_map/all_to_all | solution.py:272
  32.8 32.4 %copy-start.8 = (f32[640,224]{0,1:T(8,128)S(1)}, f32[640,224]{0,1:T(8,128)}, u32[]{:S(2)}) copy-start(f32[640,224]{0,1:T(8,128)} %param.16) | copy-start | bytes 1720324
  32.8 14.3 %collective-permute-start = (bf16[160,1792]{1,0:T(8,128)(2,1)}, bf16[160,1792]{1,0:T(8,128)(2,1)S(1)}, u32[]{:S(2)}, u32[]{:S(2)}) collective-permute-start(bf16[160,1792]{1,0:T(8,128)(2,1)} %get-tuple-element.41), channel_id=1, source_target_pairs={{0,3},{1,2},{2,1},{3,0},{4,7},{5,6},{6,5},{7,4},{8,11},{9,10},{10,... | collective-permute-start | bytes 1720328 | tf_op jit(solution)/shard_map/ppermute | solution.py:265
  35.4 12.5 %collective-permute-start.1 = (bf16[160,1792]{1,0:T(8,128)(2,1)S(1)}, bf16[160,1792]{1,0:T(8,128)(2,1)S(1)}, u32[]{:S(2)}, u32[]{:S(2)}) collective-permute-start(bf16[160,1792]{1,0:T(8,128)(2,1)S(1)} %copy-done.11), channel_id=1, source_target_pairs={{0,1},{1,0},{2,3},{3,2},{4,5},{5,4},{6,7},{7,6},{8,9},{9,8},{10,11... | collective-permute-start | bytes 1720328 | tf_op jit(solution)/shard_map/ppermute | solution.py:262
  47.2 20.9 %copy-start.12 = (bf16[160,1792]{1,0:T(8,128)(2,1)}, bf16[160,1792]{1,0:T(8,128)(2,1)S(1)}, u32[]{:S(2)}) copy-start(bf16[160,1792]{1,0:T(8,128)(2,1)S(1)} %collective-permute-done.refs_1_) | copy-start | bytes 1720324
  47.9 11.6 %collective-permute-start.2 = (bf16[160,1792]{1,0:T(8,128)(2,1)S(1)}, bf16[160,1792]{1,0:T(8,128)(2,1)S(1)}, u32[]{:S(2)}, u32[]{:S(2)}) collective-permute-start(bf16[160,1792]{1,0:T(8,128)(2,1)S(1)} %collective-permute-done.refs_1_), channel_id=1, source_target_pairs={{0,1},{1,0},{2,3},{3,2},{4,5},{5,4},{6,7},{7,6},{8,9},{9,8},{10,11... | collective-permute-start | bytes 1720328 | tf_op jit(solution)/shard_map/ppermute | solution.py:262
  49.8 16.6 %copy-start.9 = (f32[640,224]{0,1:T(8,128)S(1)}, f32[640,224]{0,1:T(8,128)}, u32[]{:S(2)}) copy-start(f32[640,224]{0,1:T(8,128)} %param.17) | copy-start | bytes 1720324
  52.2 13.0 %collective-permute-start.3 = (bf16[160,1792]{1,0:T(8,128)(2,1)}, bf16[160,1792]{1,0:T(8,128)(2,1)S(1)}, u32[]{:S(2)}, u32[]{:S(2)}) collective-permute-start(bf16[160,1792]{1,0:T(8,128)(2,1)} %get-tuple-element.46), channel_id=1, source_target_pairs={{0,3},{1,2},{2,1},{3,0},{4,7},{5,6},{6,5},{7,4},{8,11},{9,10},{10,... | collective-permute-start | bytes 1720328 | tf_op jit(solution)/shard_map/ppermute | solution.py:265
  54.0 27.8 %collective-permute-start.6 = (bf16[160,1792]{1,0:T(8,128)(2,1)}, bf16[160,1792]{1,0:T(8,128)(2,1)S(1)}, u32[]{:S(2)}, u32[]{:S(2)}) collective-permute-start(bf16[160,1792]{1,0:T(8,128)(2,1)} %get-tuple-element.45.refs_6_.refs_1_.refs_0_), channel_id=1, source_target_pairs={{0,1},{1,0},{2,3},{3,2},{4,5},{5,4},{6,7},{7,6},{8,9},{9,8},{10,11... | collective-permute-start | bytes 1720328 | tf_op jit(solution)/shard_map/ppermute | solution.py:262
  59.5 7.9 %copy-start.14 = (bf16[160,1792]{1,0:T(8,128)(2,1)}, bf16[160,1792]{1,0:T(8,128)(2,1)S(1)}, u32[]{:S(2)}) copy-start(bf16[160,1792]{1,0:T(8,128)(2,1)S(1)} %collective-permute-done.2.refs_3_) | copy-start | bytes 1720324
  65.3 2.2 copy-start.10
  65.3 19.0 %collective-permute-start.4 = (bf16[160,1792]{1,0:T(8,128)(2,1)S(1)}, bf16[160,1792]{1,0:T(8,128)(2,1)}, u32[]{:S(2)}, u32[]{:S(2)}) collective-permute-start(bf16[160,1792]{1,0:T(8,128)(2,1)S(1)} %collective-permute-done.3.refs_7_.refs_2_.refs_0_), channel_id=1, source_target_pairs={{0,1},{1,0},{2,3},{3,2},{4,5},{5,4},{6,7},{7,6},{8,9},{9,8},{10,11... | collective-permute-start | bytes 1720328 | tf_op jit(solution)/shard_map/ppermute | solution.py:262
  81.8 2.8 %copy-start.19 = (bf16[160,1792]{1,0:T(8,128)(2,1)}, bf16[160,1792]{1,0:T(8,128)(2,1)S(1)}, u32[]{:S(2)}) copy-start(bf16[160,1792]{1,0:T(8,128)(2,1)S(1)} %collective-permute-done.6.refs_3_.refs_0_) | copy-start | bytes 1720324
  81.8 17.0 %collective-permute-start.7 = (bf16[160,1792]{1,0:T(8,128)(2,1)}, bf16[160,1792]{1,0:T(8,128)(2,1)S(1)}, u32[]{:S(2)}, u32[]{:S(2)}) collective-permute-start(bf16[160,1792]{1,0:T(8,128)(2,1)} %get-tuple-element.54), channel_id=1, source_target_pairs={{0,1},{1,0},{2,3},{3,2},{4,5},{5,4},{6,7},{7,6},{8,9},{9,8},{10,11... | collective-permute-start | bytes 1720328 | tf_op jit(solution)/shard_map/ppermute | solution.py:262
  84.2 27.0 %collective-permute-start.5 = (bf16[160,1792]{1,0:T(8,128)(2,1)}, bf16[160,1792]{1,0:T(8,128)(2,1)S(1)}, u32[]{:S(2)}, u32[]{:S(2)}) collective-permute-start(bf16[160,1792]{1,0:T(8,128)(2,1)} %get-tuple-element.51), channel_id=1, source_target_pairs={{0,1},{1,0},{2,3},{3,2},{4,5},{5,4},{6,7},{7,6},{8,9},{9,8},{10,11... | collective-permute-start | bytes 1720328 | tf_op jit(solution)/shard_map/ppermute | solution.py:262
  92.3 19.0 %collective-permute-start.8 = (bf16[896,640]{1,0:T(8,128)(2,1)}, bf16[896,640]{1,0:T(8,128)(2,1)S(1)}, u32[]{:S(2)}, u32[]{:S(2)}) collective-permute-start(bf16[896,640]{1,0:T(8,128)(2,1)} %get-tuple-element.56.refs_7_), channel_id=1, source_target_pairs={{0,32},{32,0},{64,96},{96,64},{128,160},{160,128},{192,224},{224,1... | collective-permute-start | bytes 3440648 | tf_op jit(solution)/shard_map/ppermute | solution.py:268
  109.5 36.8 %collective-permute-start.10 = (bf16[160,1792]{1,0:T(8,128)(2,1)}, bf16[160,1792]{1,0:T(8,128)(2,1)S(1)}, u32[]{:S(2)}, u32[]{:S(2)}) collective-permute-start(bf16[160,1792]{1,0:T(8,128)(2,1)} %get-tuple-element.62), channel_id=1, source_target_pairs={{0,1},{1,0},{2,3},{3,2},{4,5},{5,4},{6,7},{7,6},{8,9},{9,8},{10,11... | collective-permute-start | bytes 1720328 | tf_op jit(solution)/shard_map/ppermute | solution.py:262
  111.2 4.5 %copy-start.6 = (bf16[160,1792]{1,0:T(8,128)(2,1)}, bf16[160,1792]{1,0:T(8,128)(2,1)S(1)}, u32[]{:S(2)}) copy-start(bf16[160,1792]{1,0:T(8,128)(2,1)S(1)} %collective-permute-done.5.refs_3_.refs_1_) | copy-start | bytes 1720324
  111.2 57.4 %collective-permute-start.13 = (bf16[160,1792]{1,0:T(8,128)(2,1)}, bf16[160,1792]{1,0:T(8,128)(2,1)S(1)}, u32[]{:S(2)}, u32[]{:S(2)}) collective-permute-start(bf16[160,1792]{1,0:T(8,128)(2,1)} %get-tuple-element.67.refs_2_), channel_id=1, source_target_pairs={{0,1},{1,0},{2,3},{3,2},{4,5},{5,4},{6,7},{7,6},{8,9},{9,8},{10,11... | collective-permute-start | bytes 1720328 | tf_op jit(solution)/shard_map/ppermute | solution.py:262
  111.3 1.1 copy-start.17
  115.7 26.4 %collective-permute-start.11 = (bf16[112,640]{1,0:T(8,128)(2,1)}, bf16[112,640]{1,0:T(8,128)(2,1)S(1)}, u32[]{:S(2)}, u32[]{:S(2)}) collective-permute-start(bf16[112,640]{1,0:T(8,128)(2,1)} %get-tuple-element.60.refs_2_), channel_id=1, source_target_pairs={{0,64},{32,96},{64,128},{96,160},{128,192},{160,224},{192,0},{224,... | collective-permute-start | bytes 430088 | tf_op jit(solution)/shard_map/ppermute | solution.py:268
  118.7 3.8 %copy-start.27 = (bf16[112,640]{1,0:T(8,128)(2,1)S(1)}, bf16[112,640]{1,0:T(8,128)(2,1)}, u32[]{:S(2)}) copy-start(bf16[112,640]{1,0:T(8,128)(2,1)} %get-tuple-element.65) | copy-start | bytes 430084
  120.9 39.2 %collective-permute-start.9 = (bf16[160,1792]{1,0:T(8,128)(2,1)}, bf16[160,1792]{1,0:T(8,128)(2,1)S(1)}, u32[]{:S(2)}, u32[]{:S(2)}) collective-permute-start(bf16[160,1792]{1,0:T(8,128)(2,1)} %sum_out.1.refs_6_), channel_id=1, source_target_pairs={{0,3},{1,2},{2,1},{3,0},{4,7},{5,6},{6,5},{7,4},{8,11},{9,10},{10,... | collective-permute-start | bytes 1720328 | tf_op jit(solution)/shard_map/ppermute | solution.py:265
  122.5 19.6 %collective-permute-start.12 = (bf16[112,640]{1,0:T(8,128)(2,1)S(1)}, bf16[112,640]{1,0:T(8,128)(2,1)S(1)}, u32[]{:S(2)}, u32[]{:S(2)}) collective-permute-start(bf16[112,640]{1,0:T(8,128)(2,1)S(1)} %copy-done.27), channel_id=1, source_target_pairs={{0,192},{32,224},{64,0},{96,32},{128,64},{160,96},{192,128},{224,1... | collective-permute-start | bytes 430088 | tf_op jit(solution)/shard_map/ppermute | solution.py:268
  144.9 5.6 %copy-start.25 = (bf16[224,640]{1,0:T(8,128)(2,1)S(1)}, bf16[224,640]{1,0:T(8,128)(2,1)}, u32[]{:S(2)}) copy-start(bf16[224,640]{1,0:T(8,128)(2,1)} %get-tuple-element.69) | copy-start | bytes 860164
  144.9 23.7 %collective-permute-start.15 = (bf16[224,640]{1,0:T(8,128)(2,1)}, bf16[224,640]{1,0:T(8,128)(2,1)S(1)}, u32[]{:S(2)}, u32[]{:S(2)}) collective-permute-start(bf16[224,640]{1,0:T(8,128)(2,1)} %get-tuple-element.66.refs_2_), channel_id=1, source_target_pairs={{0,64},{32,96},{64,128},{96,160},{128,192},{160,224},{192,0},{224,... | collective-permute-start | bytes 860168 | tf_op jit(solution)/shard_map/ppermute | solution.py:268
  149.4 25.6 %collective-permute-start.14 = (bf16[160,1792]{1,0:T(8,128)(2,1)}, bf16[160,1792]{1,0:T(8,128)(2,1)S(1)}, u32[]{:S(2)}, u32[]{:S(2)}) collective-permute-start(bf16[160,1792]{1,0:T(8,128)(2,1)} %sum_in.1.refs_6_), channel_id=1, source_target_pairs={{0,3},{1,2},{2,1},{3,0},{4,7},{5,6},{6,5},{7,4},{8,11},{9,10},{10,... | collective-permute-start | bytes 1720328 | tf_op jit(solution)/shard_map/ppermute | solution.py:265
  150.5 18.2 %collective-permute-start.16 = (bf16[224,640]{1,0:T(8,128)(2,1)S(1)}, bf16[224,640]{1,0:T(8,128)(2,1)}, u32[]{:S(2)}, u32[]{:S(2)}) collective-permute-start(bf16[224,640]{1,0:T(8,128)(2,1)S(1)} %copy-done.25), channel_id=1, source_target_pairs={{0,192},{32,224},{64,0},{96,32},{128,64},{160,96},{192,128},{224,1... | collective-permute-start | bytes 860168 | tf_op jit(solution)/shard_map/ppermute | solution.py:268
  163.5 19.9 %all-to-all-start.2 = ((bf16[8,40,1792]{2,1,0:T(8,128)(2,1)}), bf16[8,40,1792]{2,1,0:T(8,128)(2,1)S(1)}, u32[]{:S(2)}, u32[]{:S(2)}) async-start(bf16[8,40,1792]{2,1,0:T(8,128)(2,1)} %bitcast.18), calls=%async_computation.2 | async-start | bytes 2293760 | tf_op jit(solution)/shard_map/all_to_all | solution.py:272
  172.6 32.8 %collective-permute-start.17 = (bf16[224,640]{1,0:T(8,128)(2,1)}, bf16[224,640]{1,0:T(8,128)(2,1)S(1)}, u32[]{:S(2)}, u32[]{:S(2)}) collective-permute-start(bf16[224,640]{1,0:T(8,128)(2,1)} %get-tuple-element.70.refs_3_.refs_1_), channel_id=1, source_target_pairs={{0,192},{32,224},{64,0},{96,32},{128,64},{160,96},{192,128},{224,1... | collective-permute-start | bytes 860168 | tf_op jit(solution)/shard_map/ppermute | solution.py:268
  173.7 31.6 %collective-permute-start.18 = (bf16[224,640]{1,0:T(8,128)(2,1)}, bf16[224,640]{1,0:T(8,128)(2,1)S(1)}, u32[]{:S(2)}, u32[]{:S(2)}) collective-permute-start(bf16[224,640]{1,0:T(8,128)(2,1)} %get-tuple-element.70.refs_3_.refs_1_), channel_id=1, source_target_pairs={{0,64},{32,96},{64,128},{96,160},{128,192},{160,224},{192,0},{224,... | collective-permute-start | bytes 860168 | tf_op jit(solution)/shard_map/ppermute | solution.py:268
  183.5 4.6 %copy-start.23 = (bf16[224,640]{1,0:T(8,128)(2,1)S(1)}, bf16[224,640]{1,0:T(8,128)(2,1)}, u32[]{:S(2)}) copy-start(bf16[224,640]{1,0:T(8,128)(2,1)} %get-tuple-element.70.refs_3_.refs_1_) | copy-start | bytes 860164
  184.5 40.5 %all-to-all-start.3 = ((bf16[8,40,1792]{2,1,0:T(8,128)(2,1)}), bf16[8,40,1792]{2,1,0:T(8,128)(2,1)S(1)}, u32[]{:S(2)}, u32[]{:S(2)}) async-start(bf16[8,40,1792]{2,1,0:T(8,128)(2,1)} %bitcast.16), calls=%async_computation.3 | async-start | bytes 2293760 | tf_op jit(solution)/shard_map/all_to_all | solution.py:272
  188.1 32.9 %collective-permute-start.21 = (bf16[224,640]{1,0:T(8,128)(2,1)S(1)}, bf16[224,640]{1,0:T(8,128)(2,1)}, u32[]{:S(2)}, u32[]{:S(2)}) collective-permute-start(bf16[224,640]{1,0:T(8,128)(2,1)S(1)} %copy-done.23), channel_id=1, source_target_pairs={{0,32},{32,0},{64,96},{96,64},{128,160},{160,128},{192,224},{224,1... | collective-permute-start | bytes 860168 | tf_op jit(solution)/shard_map/ppermute | solution.py:268
  202.3 16.5 %copy-start.5 = (f32[640,224]{1,0:T(8,128)S(1)}, f32[640,224]{1,0:T(8,128)}, u32[]{:S(2)}) copy-start(f32[640,224]{1,0:T(8,128)} %get-tuple-element.77) | copy-start | bytes 1720324
  205.3 14.6 %copy-start.4 = (f32[640,224]{1,0:T(8,128)S(1)}, f32[640,224]{1,0:T(8,128)}, u32[]{:S(2)}) copy-start(f32[640,224]{1,0:T(8,128)} %get-tuple-element.78) | copy-start | bytes 1720324
  205.3 15.6 %copy-start.15 = (bf16[224,640]{1,0:T(8,128)(2,1)}, bf16[224,640]{1,0:T(8,128)(2,1)S(1)}, u32[]{:S(2)}) copy-start(bf16[224,640]{1,0:T(8,128)(2,1)S(1)} %collective-permute-done.17.refs_2_) | copy-start | bytes 860164
  205.4 15.6 %copy-start.16 = (bf16[224,640]{1,0:T(8,128)(2,1)}, bf16[224,640]{1,0:T(8,128)(2,1)S(1)}, u32[]{:S(2)}) copy-start(bf16[224,640]{1,0:T(8,128)(2,1)S(1)} %collective-permute-done.18.refs_5_) | copy-start | bytes 860164
  205.4 10.8 %collective-permute-start.19 = (bf16[112,640]{1,0:T(8,128)(2,1)S(1)}, bf16[112,640]{1,0:T(8,128)(2,1)S(1)}, u32[]{:S(2)}, u32[]{:S(2)}) collective-permute-start(bf16[112,640]{1,0:T(8,128)(2,1)S(1)} %slice.6), channel_id=1, source_target_pairs={{0,64},{32,96},{64,128},{96,160},{128,192},{160,224},{192,0},{224,... | collective-permute-start | bytes 430088 | tf_op jit(solution)/shard_map/ppermute | solution.py:268
  207.9 13.1 %collective-permute-start.22 = (bf16[224,640]{1,0:T(8,128)(2,1)S(1)}, bf16[224,640]{1,0:T(8,128)(2,1)}, u32[]{:S(2)}, u32[]{:S(2)}) collective-permute-start(bf16[224,640]{1,0:T(8,128)(2,1)S(1)} %collective-permute-done.17.refs_2_), channel_id=1, source_target_pairs={{0,32},{32,0},{64,96},{96,64},{128,160},{160,128},{192,224},{224,1... | collective-permute-start | bytes 860168 | tf_op jit(solution)/shard_map/ppermute | solution.py:268
  208.2 10.5 %collective-permute-start.20 = (bf16[112,640]{1,0:T(8,128)(2,1)S(1)}, bf16[112,640]{1,0:T(8,128)(2,1)}, u32[]{:S(2)}, u32[]{:S(2)}) collective-permute-start(bf16[112,640]{1,0:T(8,128)(2,1)S(1)} %slice.7), channel_id=1, source_target_pairs={{0,192},{32,224},{64,0},{96,32},{128,64},{160,96},{192,128},{224,1... | collective-permute-start | bytes 430088 | tf_op jit(solution)/shard_map/ppermute | solution.py:268
  209.4 11.5 %collective-permute-start.25 = (bf16[224,640]{1,0:T(8,128)(2,1)S(1)}, bf16[224,640]{1,0:T(8,128)(2,1)}, u32[]{:S(2)}, u32[]{:S(2)}) collective-permute-start(bf16[224,640]{1,0:T(8,128)(2,1)S(1)} %collective-permute-done.18.refs_5_), channel_id=1, source_target_pairs={{0,32},{32,0},{64,96},{96,64},{128,160},{160,128},{192,224},{224,1... | collective-permute-start | bytes 860168 | tf_op jit(solution)/shard_map/ppermute | solution.py:268
  216.2 4.7 %copy-start.26 = (bf16[112,640]{1,0:T(8,128)(2,1)}, bf16[112,640]{1,0:T(8,128)(2,1)S(1)}, u32[]{:S(2)}) copy-start(bf16[112,640]{1,0:T(8,128)(2,1)S(1)} %collective-permute-done.19.refs_3_) | copy-start | bytes 430084
  216.2 4.8 %collective-permute-start.23 = (bf16[112,640]{1,0:T(8,128)(2,1)S(1)}, bf16[112,640]{1,0:T(8,128)(2,1)}, u32[]{:S(2)}, u32[]{:S(2)}) collective-permute-start(bf16[112,640]{1,0:T(8,128)(2,1)S(1)} %collective-permute-done.19.refs_3_), channel_id=1, source_target_pairs={{0,32},{32,0},{64,96},{96,64},{128,160},{160,128},{192,224},{224,1... | collective-permute-start | bytes 430088 | tf_op jit(solution)/shard_map/ppermute | solution.py:268
  218.8 2.2 collective-permute-start.24
  225.0 1.0 copy-start.3
  (12 other events, 10.2 us)
